TPU v7x, 512 devices: a whole 4x8x8 slice. The times are simulated.
512 devices in a mesh: state: 8 (over x, core), member: 64 (over z, y).
Axes of the slice: x: 4, y: 8, z: 8, core: 2. Of those that a mesh axis runs over, the one named last changes fastest.
Arguments:
- state: float32 [2048, 5120], P('member', 'state'), may hold values from -6 to 6
- obs_values: float32 [2, 384], replicated, may hold values from -8 to 8
- noise_var: float32 [2, 384], replicated, may hold values from 0.3 to 3
- obs_rows: int32 [2, 384], replicated, may hold values from 0 to 639
- owner: int32 [2, 3], replicated, may hold values from 0 to 7
Outputs:
- analysis: float32 [2048, 5120], P('member', 'state')
All inputs are finite; a program needn't handle non-finite values.
Results may differ from a plain program's by a relative error of at most 0.0003.
Values sent between devices are 32-bit elements; how exact they have to be, the bound alone decides.
A program may use at most 64 MiB of HBM per device.

v0:
```python
import jax
import jax.numpy as jnp
from jax import lax
from jax.sharding import PartitionSpec as P


def from_root(x, axis, root):
    mine = lax.axis_index(axis) == root
    return lax.psum(jnp.where(mine, x, jnp.zeros_like(x)), axis)


def full_dot(left, right):
    return jnp.dot(left, right, precision=lax.Precision.HIGHEST, preferred_element_type=jnp.float32)


def solve_gram(factor, right):
    half = lax.linalg.triangular_solve(factor, right, left_side=True, lower=True)
    return lax.linalg.triangular_solve(factor, half, left_side=True, lower=True, transpose_a=True)


def tile_rows(state, picks, source):
    local_rows = jnp.take(state, picks, axis=1)
    return from_root(local_rows, "state", source)


def owner_rows(state, picks, owners_block):
    num_tiles = owners_block.shape[0]
    tile_width = picks.shape[0] // num_tiles
    pieces = []
    for tile in range(num_tiles):
        pieces.append(
            tile_rows(state, picks[tile * tile_width : (tile + 1) * tile_width], owners_block[tile])
        )
    return jnp.concatenate(pieces, axis=1)


def analyse(current, observed, target, noise):
    count = observed.shape[0] * lax.axis_size("member")
    row_sums, obs_sums = lax.psum((jnp.sum(current, axis=0), jnp.sum(observed, axis=0)), "member")
    row_mean = row_sums / count
    obs_mean = obs_sums / count
    row_anom = current - row_mean[None, :]
    obs_anom = observed - obs_mean[None, :]
    cross_sum, gram_sum = lax.psum(
        (full_dot(obs_anom.T, row_anom), full_dot(obs_anom.T, obs_anom)), "member"
    )
    cross = cross_sum / (count - 1.0)
    innov_cov = gram_sum / (count - 1.0) + jnp.diag(noise)
    factor = jnp.linalg.cholesky(innov_cov)
    weights = solve_gram(factor, (target - obs_mean)[:, None])
    transformed = solve_gram(factor, obs_anom.T)
    shift = full_dot(weights.T, cross)
    return row_mean[None, :] + shift + row_anom - 0.5 * full_dot(transformed.T, cross)


def shards(state, obs_values, noise_var, obs_rows, owner):
    num_blocks = obs_rows.shape[0]
    current = state
    for block in range(num_blocks):
        observed = owner_rows(current, obs_rows[block], owner[block])
        current = analyse(current, observed, obs_values[block], noise_var[block])
    return current


def solution(mesh):
    placed = (P("member", "state"), P(), P(), P(), P())
    return jax.shard_map(
        shards, mesh=mesh, in_specs=placed, out_specs=P("member", "state"), check_vma=False
    )
```

profile of v0, /device:TPU:1, one launch (start us, length us, event | category | flops | bytes accessed | tf_op | source)
XLA Modules:
  0.0 888.4 jit_solution(12492912594317526114)
XLA Ops:
  6.5 0.8 compare_and_fusion.2
  7.3 1.1 copy.16
  8.4 0.7 fusion.154
  13.2 29.2 %all-reduce.6 = (f32[32,128]{0,1:T(8,128)S(1)}, f32[32,128]{0,1:T(8,128)S(1)}, f32[32,128]{0,1:T(8,128)S(1)}) all-reduce(f32[32,128]{0,1:T(8,128)S(1)} %bitcast_select_fusion.3, f32[32,128]{0,1:T(8,128)S(1)} %bitcast_select_fusion.4, f32[32,128]{0,1:T(8,128)S(1)} %bitcast_select_fusion.5), channel_id=1, replica_groups=mesh['state'=8,'member'=64] {'state'}, use_global_device_ids=true, to_apply=%region_4.6 | all-reduce | flops 12288 | bytes 98304 | tf_op jit(solution)/shard_map/psum | solution.py:9
  42.6 0.8 copy-done.4
  43.4 0.7 copy-done.6
  44.1 120.6 %all-reduce.2 = (f32[640]{0:T(1024)S(1)}, f32[384]{0:T(512)S(1)}) all-reduce(f32[640]{0:T(1024)S(1)} %reduce_sum.36, f32[384]{0:T(512)S(1)} %fusion.103), channel_id=1, replica_groups=mesh['state'=8,'member'=64] {'member'}, use_global_device_ids=true, to_apply=%region_1.2 | all-reduce | flops 1024 | bytes 8192 | tf_op jit(solution)/shard_map/psum | solution.py:39
  164.8 1.5 fusion.80
  166.3 2.0 fusion.36
  170.5 0.7 copy-done.7
  171.2 174.0 %all-reduce.12.cloned.1.call-done = (f32[384,640]{1,0:T(8,128)}, f32[384,384]{0,1:T(8,128)}) async-done(((f32[384,640]{1,0:T(8,128)}, f32[384,384]{0,1:T(8,128)}), (f32[384,640]{1,0:T(8,128)}, f32[384,384]{0,1:T(8,128)})) %all-reduce.12.cloned.1.call-update) | async-done | bytes 1572880 | tf_op jit(solution)/shard_map/psum | solution.py:44
  345.3 1.1 select_add_fusion.1
  346.6 0.8 copy-done.2
  347.6 11.7 %cholesky.208 = f32[128,128]{1,0:T(8,128)S(1)} custom-call(f32[128,128]{1,0:T(8,128)S(1)} %cholesky.310), custom_call_target="Cholesky" | custom-call | tf_op jit(solution)/shard_map/jit(cholesky)/cholesky | solution.py:49
  359.4 9.8 %custom-call.32 = f32[1,128,128]{1,2,0:T(8,128)S(1)} custom-call(f32[1,128,128]{2,1,0:T(8,128)S(1)} %get-tuple-element.138), custom_call_target="InvertDiagBlocksLowerTriangular" | custom-call | tf_op jit(solution)/shard_map/jit(cholesky)/cholesky | solution.py:49
  369.7 11.7 %cholesky.227 = f32[128,128]{1,0:T(8,128)S(1)} custom-call(f32[128,128]{1,0:T(8,128)S(1)} %cholesky.314), custom_call_target="Cholesky" | custom-call | tf_op jit(solution)/shard_map/jit(cholesky)/cholesky | solution.py:49
  381.5 0.7 compare_reduce_fusion.4
  382.8 10.0 %custom-call.33 = f32[1,128,128]{1,2,0:T(8,128)S(1)} custom-call(f32[1,128,128]{2,1,0:T(8,128)S(1)} %get-tuple-element.135), custom_call_target="InvertDiagBlocksLowerTriangular" | custom-call | tf_op jit(solution)/shard_map/jit(cholesky)/cholesky | solution.py:49
  393.3 11.7 %cholesky.246 = f32[128,128]{1,0:T(8,128)S(1)} custom-call(f32[128,128]{1,0:T(8,128)S(1)} %convolution_subtract_fusion.3), custom_call_target="Cholesky" | custom-call | tf_op jit(solution)/shard_map/jit(cholesky)/cholesky | solution.py:49
  405.0 0.7 compare_reduce_fusion.3
  407.8 5.9 while.16
  408.4 1.4 bitcast_dynamic-update-slice_fusion.4
  410.4 1.4 bitcast_dynamic-update-slice_fusion.4
  412.4 1.4 bitcast_dynamic-update-slice_fusion.4
  413.8 29.5 %custom-call.35 = f32[3,128,128]{1,2,0:T(8,128)S(1)} custom-call(f32[3,128,128]{2,1,0:T(8,128)S(1)} %get-tuple-element.68), custom_call_target="InvertDiagBlocksLowerTriangular" | custom-call | tf_op jit(solution)/shard_map/triangular_solve/custom-call.6 | solution.py:18
  445.2 0.7 convolution_reduce_fusion.1
  447.9 0.7 fusion.155
  448.8 0.7 gather_fusion.4
  451.0 26.7 %all-reduce.5 = (f32[32,128]{0,1:T(8,128)S(1)}, f32[32,128]{0,1:T(8,128)S(1)}, f32[32,128]{0,1:T(8,128)S(1)}) all-reduce(f32[32,128]{0,1:T(8,128)S(1)} %get-tuple-element.165, f32[32,128]{0,1:T(8,128)S(1)} %get-tuple-element.166, f32[32,128]{0,1:T(8,128)S(1)} %bitcast_select_fusion.2), channel_id=1, replica_groups=mesh['state'=8,'member'=64] {'state'}, use_global_device_ids=true, to_apply=%region_19.26 | all-reduce | flops 12288 | bytes 98304 | tf_op jit(solution)/shard_map/psum | solution.py:9
  477.9 115.9 %all-reduce.1 = (f32[640]{0:T(1024)S(1)}, f32[384]{0:T(512)S(1)}) all-reduce(f32[640]{0:T(1024)S(1)} %get-tuple-element.161, f32[384]{0:T(512)S(1)} %fusion.102), channel_id=1, replica_groups=mesh['state'=8,'member'=64] {'member'}, use_global_device_ids=true, to_apply=%region_16.0 | all-reduce | flops 1024 | bytes 8192 | tf_op jit(solution)/shard_map/psum | solution.py:39
  593.8 1.5 fusion.77
  595.3 2.0 fusion.34
  597.3 179.9 %all-reduce.10.cloned.1.call-done = (f32[384,640]{1,0:T(8,128)}, f32[384,384]{0,1:T(8,128)}) async-done(((f32[384,640]{1,0:T(8,128)}, f32[384,384]{0,1:T(8,128)}), (f32[384,640]{1,0:T(8,128)}, f32[384,384]{0,1:T(8,128)})) %all-reduce.10.cloned.1.call-update) | async-done | bytes 1572880 | tf_op jit(solution)/shard_map/psum | solution.py:44
  777.3 1.1 select_add_fusion
  778.6 0.8 copy-done.3
  779.6 11.7 %cholesky.261 = f32[128,128]{1,0:T(8,128)S(1)} custom-call(f32[128,128]{1,0:T(8,128)S(1)} %cholesky.318), custom_call_target="Cholesky" | custom-call | tf_op jit(solution)/shard_map/jit(cholesky)/cholesky | solution.py:49
  791.4 9.8 %custom-call.38 = f32[1,128,128]{1,2,0:T(8,128)S(1)} custom-call(f32[1,128,128]{2,1,0:T(8,128)S(1)} %get-tuple-element.131), custom_call_target="InvertDiagBlocksLowerTriangular" | custom-call | tf_op jit(solution)/shard_map/jit(cholesky)/cholesky | solution.py:49
  801.7 11.7 %cholesky.280 = f32[128,128]{1,0:T(8,128)S(1)} custom-call(f32[128,128]{1,0:T(8,128)S(1)} %cholesky.322), custom_call_target="Cholesky" | custom-call | tf_op jit(solution)/shard_map/jit(cholesky)/cholesky | solution.py:49
  813.5 0.7 compare_reduce_fusion.1
  814.8 10.0 %custom-call.39 = f32[1,128,128]{1,2,0:T(8,128)S(1)} custom-call(f32[1,128,128]{2,1,0:T(8,128)S(1)} %get-tuple-element.128), custom_call_target="InvertDiagBlocksLowerTriangular" | custom-call | tf_op jit(solution)/shard_map/jit(cholesky)/cholesky | solution.py:49
  825.3 11.7 %cholesky.299 = f32[128,128]{1,0:T(8,128)S(1)} custom-call(f32[128,128]{1,0:T(8,128)S(1)} %convolution_subtract_fusion.2), custom_call_target="Cholesky" | custom-call | tf_op jit(solution)/shard_map/jit(cholesky)/cholesky | solution.py:49
  839.6 6.3 while.17
  840.3 1.4 bitcast_dynamic-update-slice_fusion.5
  842.4 1.4 bitcast_dynamic-update-slice_fusion.5
  844.4 1.4 bitcast_dynamic-update-slice_fusion.5
  845.9 29.5 %custom-call.41 = f32[3,128,128]{1,2,0:T(8,128)S(1)} custom-call(f32[3,128,128]{2,1,0:T(8,128)S(1)} %get-tuple-element.72), custom_call_target="InvertDiagBlocksLowerTriangular" | custom-call | tf_op jit(solution)/shard_map/triangular_solve/custom-call.6 | solution.py:18
  877.3 0.7 convolution_reduce_fusion
  880.0 1.4 fusion
  (138 shorter events, 21.3 us)
Async XLA Ops:
  6.5 338.7 %all-reduce.12.cloned.1.call-start = ((), (), s32[]{:S(2)}) async-start(), calls=%async_computation.1 | async-start | bytes 3145728 | tf_op jit(solution)/shard_map/psum | solution.py:44
  7.3 1.1 copy-start.5
  42.5 0.9 copy-start.4
  43.4 0.7 copy-start.6
  168.3 609.0 %all-reduce.10.cloned.1.call-start = ((), (), s32[]{:S(2)}) async-start(), calls=%async_computation | async-start | bytes 3145728 | tf_op jit(solution)/shard_map/psum | solution.py:44
  170.5 0.7 copy-start.7
  346.4 1.1 copy-start.2
  407.8 37.4 %copy-start = (f32[384,640]{1,0:T(8,128)S(1)}, f32[384,640]{1,0:T(8,128)}, u32[]{:S(2)}) copy-start(f32[384,640]{1,0:T(8,128)} %get-tuple-element.101) | copy-start | bytes 2949124
  778.4 1.1 copy-start.3
  839.6 37.7 %copy-start.1 = (f32[384,640]{1,0:T(8,128)S(1)}, f32[384,640]{1,0:T(8,128)}, u32[]{:S(2)}) copy-start(f32[384,640]{1,0:T(8,128)} %get-tuple-element.99) | copy-start | bytes 2949124
Sparse Core Ops, SparseCore 0:
  168.4 176.8 all-reduce.11
  597.4 179.7 all-reduce.9
where the time goes:
time: 895 us; the launch traced here: 888 us
  waiting for transfers between devices  354 us (40%)
  blocking collectives  292 us (33%)
  other arithmetic  177 us (20%)
  local copies, waits for them, and re-layouts  22.6 us (3%)
  between operations  21.9 us (2%)
  matrix products  20.2 us (2%)
    psum x2, waiting for transfers between devices, analyse(): lax.psum((full_dot(obs_anom.T, row_anom), full_dot(obs_anom.T, obs_anom))...  354 us
    psum x2, blocking collectives, analyse(): lax.psum((jnp.sum(current, axis=0), jnp.sum(observed, axis=0)), 'member')  236 us
    another operation x22, other arithmetic, analyse(): factor = jnp.linalg.cholesky(innov_cov)  114 us
    another operation x5, other arithmetic, solve_gram(): lax.linalg.triangular_solve(factor, half, left_side=True, lower=True, tra...  59.1 us
    psum x2, blocking collectives, from_root(): return lax.psum(jnp.where(mine, x, jnp.zeros_like(x)), axis)  55.9 us
  transfers between devices with their start and end apart: 2, of which 2 were waited for; matrix products, arithmetic and copies ran while one was open for 0% of the time, Pallas kernels for 0%

commit v1 on v0

v1 whole, which is shorter than its diff:
```python
import functools

import jax
import jax.numpy as jnp
from jax import lax
from jax.experimental import pallas as pl
from jax.experimental.pallas import tpu as pltpu
from jax.sharding import PartitionSpec as P

MESH = pl.DeviceIdType.MESH
F32 = jnp.float32
HIGHEST = lax.Precision.HIGHEST
SIDE = 8
OBS = 384
ALL = 2 * OBS
ROWS = 640
MINE = 32
MEMBERS = 2048
BLOCKS = [(i, j) for i in range(6) for j in range(i + 1)]


def dot(a, b, over=(1, 0)):
    return lax.dot_general(
        a, b, (((over[0],), (over[1],)), ((), ())), precision=HIGHEST, preferred_element_type=F32
    )


def total(slots, own):
    out = own
    for k in range(1, SIDE):
        out = out + slots[k]
    return out


def gather_kernel(
    x_ref, l_ref, oa_ref, mean_ref, gram_ref, cross_ref,
    t_in, t_z, t_y, t_s, l_src, l_in, l_mine, l_all, anom,
    g_part, g_one, g_red, g_two, c_part, c_one, c_red, c_two, c_sum,
    t_send, t_recv, l_send, l_recv, g_send, g_recv, x_send, x_recv, c_send, c_recv,
):
    s = lax.axis_index("state")
    m = lax.axis_index("member")
    z, y = lax.div(m, SIDE), lax.rem(m, SIDE)
    xpos, core = lax.div(s, 2), lax.rem(s, 2)

    def hop(v, k):
        return lax.rem(v + k, SIDE)

    def peer(axis, k):
        if axis == "z":
            return (s, hop(z, k) * SIDE + y)
        if axis == "y":
            return (s, z * SIDE + hop(y, k))
        return (hop(s, k), m)

    barrier = pltpu.get_barrier_semaphore()
    for axis in ("z", "y", "s"):
        for k in range(1, SIDE):
            pl.semaphore_signal(barrier, inc=1, device_id=peer(axis, k), device_id_type=MESH)

    def copy(src, dst, send, recv, where):
        c = pltpu.make_async_remote_copy(
            src_ref=src, dst_ref=dst, send_sem=send, recv_sem=recv, device_id=where, device_id_type=MESH
        )
        c.start()
        return c

    def arrive(copies):
        for c in copies:
            c.wait_recv()

    started = []

    def fan(axis, src, dst, send, recv):
        out = [copy(src(k), dst(k), send.at[k], recv.at[k], peer(axis, k)) for k in range(1, SIDE)]
        started.extend(out)
        return out

    x = x_ref[...]
    lrows = l_ref[...]
    t_in[...] = jnp.zeros_like(t_in)
    sx = jnp.sum(x, axis=0, keepdims=True)
    sl = jnp.sum(lrows, axis=0, keepdims=True)
    for b in range(5):
        t_in[8 + b : 9 + b, :] = sx[:, 128 * b : 128 * b + 128]
    for b in range(6):
        t_in[b : b + 1, :] = sl[:, 128 * b : 128 * b + 128]
        l_src[4 * b : 4 * b + 4] = lrows[:, 128 * b : 128 * b + 128].reshape(4, 8, 128)
    pl.semaphore_wait(barrier, 3 * (SIDE - 1))

    tz = fan("z", lambda k: t_in, lambda k: t_z.at[k], t_send.at[0], t_recv.at[0])
    ls = fan("s", lambda k: l_src.at[pl.ds(3 * hop(s, k), 3)], lambda k: l_in.at[k], l_send.at[0], l_recv.at[0])
    arrive(ls)
    l_mine[...] = total(l_in, l_src[pl.ds(3 * s, 3)])
    l_all[pl.ds(3 * s, 3)] = l_mine[...]
    la = fan("s", lambda k: l_mine, lambda k: l_all.at[pl.ds(3 * s, 3)], l_send.at[1], l_recv.at[1])
    arrive(tz)
    t_y[0] = total(t_z, t_in[...])
    ty = fan("y", lambda k: t_y.at[0], lambda k: t_y.at[k], t_send.at[1], t_recv.at[1])
    arrive(ty)
    sums = total(t_y, t_y[0])
    t_s[0] = sums[0:8]
    ts = fan("s", lambda k: t_s.at[0], lambda k: t_s.at[k], t_send.at[2], t_recv.at[2])
    xmean = sums[8:16] / MEMBERS
    for b in range(5):
        anom[:, 128 * b : 128 * b + 128] = x[:, 128 * b : 128 * b + 128] - xmean[b : b + 1]
    arrive(la)
    arrive(ts)
    omean = total(t_s, t_s[0]) / MEMBERS
    mean_ref[...] = omean
    for b in range(6):
        oa_ref[:, 128 * b : 128 * b + 128] = l_all[4 * b : 4 * b + 4].reshape(MINE, 128) - omean[b : b + 1]

    for i in range(6):
        band = dot(oa_ref[:, 128 * i : 128 * i + 128], oa_ref[:, 0 : 128 * i + 128], (0, 0))
        for j in range(i + 1):
            at = 16 * BLOCKS.index((i, j))
            g_part[at : at + 16] = band[:, 128 * j : 128 * j + 128].reshape(16, 8, 128)
    g_part[336:384] = jnp.zeros((48, 8, 128), F32)

    gbase = s * 48
    order = (("z", z, "y", y), ("y", y, "z", z))
    g1 = []
    for h, (first, a, second, b) in enumerate(order):
        g1.append(
            fan(
                first,
                lambda k: g_part.at[pl.ds(gbase + 24 * h + 3 * hop(a, k), 3)],
                lambda k: g_one.at[h, k],
                g_send.at[h, 0],
                g_recv.at[h, 0],
            )
        )
    for i in range(6):
        band = dot(oa_ref[:, 128 * i : 128 * i + 128], anom[...], (0, 0))
        for j in range(5):
            at = 96 * j + 16 * i
            c_part[at : at + 16] = band[:, 128 * j : 128 * j + 128].reshape(16, 8, 128)
    c_part[480:512] = jnp.zeros((32, 8, 128), F32)

    g2 = []
    for h, (first, a, second, b) in enumerate(order):
        arrive(g1[h])
        g_two[h, 0] = total(g_one.at[h], g_part[pl.ds(gbase + 24 * h + 3 * a, 3)])
        g2.append(
            fan(second, lambda k: g_two.at[h, 0], lambda k: g_two.at[h, k], g_send.at[h, 1], g_recv.at[h, 1])
        )
    g3 = []
    for h, (first, a, second, b) in enumerate(order):
        arrive(g2[h])
        g_red[h] = total(g_two.at[h], g_two[h, 0])
        spot = pl.ds(gbase + 24 * h + 3 * a, 3)
        gram_ref[spot] = g_red[h]
        g3.append(
            fan(first, lambda k: g_red.at[h], lambda k: gram_ref.at[spot], g_send.at[h, 2], g_recv.at[h, 2])
        )
    arrive(g3[0])
    arrive(g3[1])
    mine = pl.ds(gbase, 48)
    gx = []
    for k in range(1, 4):
        where = (lax.rem(xpos + k, 4) * 2 + core, m)
        gx.append(copy(gram_ref.at[mine], gram_ref.at[mine], x_send.at[k], x_recv.at[k], where))
    started.extend(gx)
    gc = []
    for k in range(4):
        if k > 0:
            gx[k - 1].wait_recv()
        got = pl.ds((lax.rem(xpos + 4 - k, 4) * 2 + core) * 48, 48)
        gc.append(copy(gram_ref.at[got], gram_ref.at[got], x_send.at[4 + k], x_recv.at[4 + k], (s + 1 - 2 * core, m)))
    started.extend(gc)

    c1 = []
    for h, (first, a, second, b) in enumerate(order):
        c1.append(
            fan(
                first,
                lambda k: c_part.at[pl.ds(256 * h + 32 * hop(a, k), 32)],
                lambda k: c_one.at[h, k],
                c_send.at[h, 0],
                c_recv.at[h, 0],
            )
        )
    c2 = []
    for h, (first, a, second, b) in enumerate(order):
        arrive(c1[h])
        c_red[h] = total(c_one.at[h], c_part[pl.ds(256 * h + 32 * a, 32)])
        c2.append(
            fan(
                second,
                lambda k: c_red.at[h, pl.ds(4 * hop(b, k), 4)],
                lambda k: c_two.at[h, k],
                c_send.at[h, 1],
                c_recv.at[h, 1],
            )
        )
    c3 = []
    for h, (first, a, second, b) in enumerate(order):
        arrive(c2[h])
        c_two[h, 0] = total(c_two.at[h], c_red[h, pl.ds(4 * b, 4)])
        spot = pl.ds(4 * b, 4)
        c_sum[h, spot] = c_two[h, 0]
        c3.append(
            fan(second, lambda k: c_two.at[h, 0], lambda k: c_sum.at[h, spot], c_send.at[h, 2], c_recv.at[h, 2])
        )
    c4 = []
    for h, (first, a, second, b) in enumerate(order):
        arrive(c3[h])
        spot = pl.ds(256 * h + 32 * a, 32)
        cross_ref[spot] = c_sum[h]
        c4.append(
            fan(first, lambda k: c_sum.at[h], lambda k: cross_ref.at[spot], c_send.at[h, 3], c_recv.at[h, 3])
        )
    arrive(gc)
    arrive(c4[0])
    arrive(c4[1])
    for c in started:
        c.wait_send()


def gather_all(x, picked):
    dma = pltpu.SemaphoreType.DMA
    tiles = lambda *lead: pltpu.VMEM((*lead, 8, 128), F32)
    return pl.pallas_call(
        gather_kernel,
        out_shape=(
            jax.ShapeDtypeStruct((MINE, ALL), F32),
            jax.ShapeDtypeStruct((8, 128), F32),
            jax.ShapeDtypeStruct((384, 8, 128), F32),
            jax.ShapeDtypeStruct((512, 8, 128), F32),
        ),
        in_specs=[pl.BlockSpec(memory_space=pltpu.VMEM)] * 2,
        out_specs=[pl.BlockSpec(memory_space=pltpu.VMEM)] * 4,
        scratch_shapes=[
            pltpu.VMEM((16, 128), F32), pltpu.VMEM((SIDE, 16, 128), F32), pltpu.VMEM((SIDE, 16, 128), F32), tiles(SIDE),
            tiles(24), tiles(SIDE, 3), tiles(3), tiles(24), pltpu.VMEM((MINE, ROWS), F32),
            tiles(384), tiles(2, SIDE, 3), tiles(2, 3), tiles(2, SIDE, 3),
            tiles(512), tiles(2, SIDE, 32), tiles(2, 32), tiles(2, SIDE, 4), tiles(2, 32),
            dma((3, SIDE)), dma((3, SIDE)), dma((2, SIDE)), dma((2, SIDE)), dma((2, 3, SIDE)), dma((2, 3, SIDE)),
            dma((SIDE,)), dma((SIDE,)), dma((2, 4, SIDE)), dma((2, 4, SIDE)),
        ],
        compiler_params=pltpu.CompilerParams(
            collective_id=0, has_side_effects=True, vmem_limit_bytes=40 * 2**20
        ),
    )(x, picked)


def solve(factor, right):
    half = lax.linalg.triangular_solve(factor, right, left_side=True, lower=True)
    return lax.linalg.triangular_solve(factor, half, left_side=True, lower=True, transpose_a=True)


def shards(state, obs_values, noise_var, obs_rows, owner):
    s = lax.axis_index("state")
    held = jnp.repeat(owner.reshape(-1) == s, 128)
    picked = jnp.where(held[None, :], jnp.take(state, obs_rows.reshape(-1), axis=1), 0.0)
    oa, means, gram, cross = gather_all(state, picked)
    scale = 1.0 / (MEMBERS - 1.0)
    rows = []
    parts = gram[:336].reshape(21, 128, 128)
    for i in range(6):
        row = []
        for j in range(6):
            row.append(parts[BLOCKS.index((i, j))] if j <= i else parts[BLOCKS.index((j, i))].T)
        rows.append(jnp.concatenate(row, axis=1))
    gram = jnp.concatenate(rows, axis=0) * scale
    cross = cross[:480].reshape(5, ALL, 128).transpose(1, 0, 2).reshape(ALL, ROWS) * scale
    omean = means[:6].reshape(ALL)
    c12, c21 = gram[:OBS, OBS:], gram[OBS:, :OBS]
    gap = obs_values.reshape(-1) - omean
    f1 = jnp.linalg.cholesky(gram[:OBS, :OBS] + jnp.diag(noise_var[0]))
    u = solve(f1, c12)
    f = 0.75 * c21 + 0.25 * dot(u * noise_var[0][:, None], jnp.eye(OBS, dtype=F32), (0, 0))
    f2 = jnp.linalg.cholesky(gram[OBS:, OBS:] - dot(f, u) + jnp.diag(noise_var[1]))
    g1, g2 = gap[None, :OBS], gap[None, OBS:]
    o1, o2 = oa[:, :OBS], oa[:, OBS:]
    b1 = g1 - 0.5 * o1
    b2 = g2 - 0.5 * o2 - dot(g1 - 0.25 * o1, u)
    q2 = solve(f2, b2.T).T
    q1 = solve(f1, (b1 - dot(q2, f)).T).T
    return state + dot(q1, cross[:OBS]) + dot(q2, cross[OBS:])


def solution(mesh):
    placed = (P("member", "state"), P(), P(), P(), P())
    return jax.shard_map(
        shards, mesh=mesh, in_specs=placed, out_specs=P("member", "state"), check_vma=False
    )
```

time: 895 us -> 389 us (0.43)
  waiting for transfers between devices: 354 us -> 0 us
  blocking collectives: 292 us -> 0 us
  Pallas kernels: 0 us -> 117 us
  local copies, waits for them, and re-layouts: 22.6 us -> 57 us
  between operations: 21.9 us -> 4.91 us
    psum x2 -> x0, waiting for transfers between devices: 354 us -> none  [analyse(): lax.psum((full_dot(obs_anom.T, row_anom), full_dot(obs_anom.T, obs_anom))...]
    psum x4 -> x0, blocking collectives: 292 us -> none  [the longest x2 236 us: analyse(): lax.psum((jnp.sum(current, axis=0), jnp.sum(observed, axis=0)), 'member')]
    pallas_call x0 -> x1, Pallas kernels: none -> 117 us  [gather_all(): pl.pallas_call(gather_kernel, out_shape=(jax.ShapeDtypeStruct((MINE, ALL)...]
    unnamed x17 -> x69, local copies, waits for them, and re-layouts: 4.81 us -> 28.2 us
    another operation x27 -> x26, other arithmetic: 173 us -> 175 us  [the longest x5 61.6 us: solve(): lax.linalg.triangular_solve(factor, half, left_side=True, lower=True, tra...]
  transfers between devices with their start and end apart: 2 -> 0, of which waited for: 2 -> 0; matrix products, arithmetic and copies ran while one was open for 0% -> 0% of each run, Pallas kernels for 0% -> 0%
where the time goes in v1:
time: 389 us; the launch traced here: 384 us
  other arithmetic  180 us (46%)
  Pallas kernels  117 us (30%)
  local copies, waits for them, and re-layouts  57 us (15%)
  matrix products  24.8 us (6%)
  between operations  4.91 us (1%)
    pallas_call x1, Pallas kernels, gather_all(): pl.pallas_call(gather_kernel, out_shape=(jax.ShapeDtypeStruct((MINE, ALL)...  117 us
    another operation x5, other arithmetic, solve(): lax.linalg.triangular_solve(factor, half, left_side=True, lower=True, tra...  61.6 us
    another operation x11, other arithmetic, shards(): jnp.linalg.cholesky(gram[OBS:, OBS:] - dot(f, u) + jnp.diag(noise_var[1]))  57.1 us
    another operation x10, other arithmetic, shards(): f1 = jnp.linalg.cholesky(gram[:OBS, :OBS] + jnp.diag(noise_var[0]))  56.4 us
    unnamed x69, local copies, waits for them, and re-layouts  28.2 us
    another operation x29, local copies, waits for them, and re-layouts, solve(): lax.linalg.triangular_solve(factor, half, left_side=True, lower=True, tra...  15.8 us
    dot_general x6, matrix products, dot(): lax.dot_general(a, b, (((over[0],), (over[1],)), ((), ())), precision=HIG...  8.25 us

profile of v1, /device:TPU:1, one launch (start us, length us, event | category | flops | bytes accessed | tf_op | source)
XLA Modules:
  0.0 384.3 jit_solution(932661439365993355)
XLA Ops:
  0.0 1.0 copy.81
  1.8 1.6 gather_fusion
  5.1 0.9 copy-done
  6.0 117.2 %shard_map.55 = (f32[32,768]{1,0:T(8,128)S(1)}, f32[8,128]{1,0:T(8,128)S(1)}, f32[384,8,128]{2,1,0:T(8,128)S(1)}, f32[512,8,128]{2,1,0:T(8,128)S(1)}) custom-call(f32[32,640]{1,0:T(8,128)S(1)} %copy-done, f32[32,768]{1,0:T(8,128)S(1)} %select_bitcast_fusion.l_ref), custom_call_target="tpu_custom_call" | custom-call | tf_op jit(solution)/shard_map/pallas_call | solution.py:224
  123.1 1.4 slice_multiply_fusion
  124.6 3.0 copy.121
  127.6 2.9 fusion.99
  155.9 1.9 broadcast_multiply_fusion
  157.9 1.0 copy.104
  158.9 1.2 fusion.5
  160.1 0.8 copy-done.10
  160.9 11.7 %cholesky.208 = f32[128,128]{1,0:T(8,128)S(1)} custom-call(f32[128,128]{1,0:T(8,128)S(1)} %cholesky.310), custom_call_target="Cholesky" | custom-call | tf_op jit(solution)/shard_map/jit(cholesky)/cholesky | solution.py:271
  172.8 9.8 %custom-call.30 = f32[1,128,128]{1,2,0:T(8,128)S(1)} custom-call(f32[1,128,128]{2,1,0:T(8,128)S(1)} %get-tuple-element.147), custom_call_target="InvertDiagBlocksLowerTriangular" | custom-call | tf_op jit(solution)/shard_map/jit(cholesky)/cholesky | solution.py:271
  182.6 1.2 fusion.22
  183.9 1.2 convolution_subtract_fusion.6
  185.1 11.9 %cholesky.227 = f32[128,128]{1,0:T(8,128)S(1)} custom-call(f32[128,128]{1,0:T(8,128)S(1)} %cholesky.314), custom_call_target="Cholesky" | custom-call | tf_op jit(solution)/shard_map/jit(cholesky)/cholesky | solution.py:271
  197.2 9.8 %custom-call.31 = f32[1,128,128]{1,2,0:T(8,128)S(1)} custom-call(f32[1,128,128]{2,1,0:T(8,128)S(1)} %get-tuple-element.145), custom_call_target="InvertDiagBlocksLowerTriangular" | custom-call | tf_op jit(solution)/shard_map/jit(cholesky)/cholesky | solution.py:271
  207.3 1.2 convolution_subtract_fusion.8
  208.5 11.7 %cholesky.246 = f32[128,128]{1,0:T(8,128)S(1)} custom-call(f32[128,128]{1,0:T(8,128)S(1)} %convolution_subtract_fusion.8), custom_call_target="Cholesky" | custom-call | tf_op jit(solution)/shard_map/jit(cholesky)/cholesky | solution.py:271
  223.6 1.1 select_select_fusion.1
  224.7 6.4 %while.10 = (s32[]{:T(128)}, f32[384,384]{0,1:T(8,128)S(1)}, s32[3,2]{0,1:T(2,128)S(1)}, f32[3,128,128]{2,1,0:T(8,128)S(1)}, s32[]{:T(128)}) while((s32[]{:T(128)}, f32[384,384]{0,1:T(8,128)S(1)}, s32[3,2]{0,1:T(2,128)S(1)}, f32[3,128,128]{2,1,0:T(8,128)S(1)}, s32[]{:T(128)}) %tuple.86), condition=%wide.while_cond.1.clone, body=%wide.while_body.1.clone.sunk | while | flops 2 | bytes 393329 | solution.py:250
  225.4 1.3 dynamic-slice.23
  227.6 1.3 dynamic-slice.23
  229.7 1.3 dynamic-slice.23
  231.2 29.9 %custom-call.37 = f32[3,128,128]{1,2,0:T(8,128)S(1)} custom-call(f32[3,128,128]{2,1,0:T(8,128)S(1)} %get-tuple-element.55), custom_call_target="InvertDiagBlocksLowerTriangular" | custom-call | tf_op jit(solution)/shard_map/triangular_solve/custom-call.8 | solution.py:250
  263.1 0.8 convolution_subtract_fusion.3
  264.3 1.0 fusion.57
  265.3 1.7 copy.117
  267.0 1.3 convolution_subtract_fusion.2
  268.4 1.0 fusion.53
  269.4 1.8 copy.116
  271.1 1.5 convolution_subtract_fusion.1
  273.1 1.8 fusion.1
  274.9 0.8 copy-done.7
  275.7 1.3 fusion
  277.3 11.7 %cholesky.261 = f32[128,128]{1,0:T(8,128)S(1)} custom-call(f32[128,128]{1,0:T(8,128)S(1)} %cholesky.318), custom_call_target="Cholesky" | custom-call | tf_op jit(solution)/shard_map/jit(cholesky)/cholesky | solution.py:274
  289.1 10.0 %custom-call.32 = f32[1,128,128]{1,2,0:T(8,128)S(1)} custom-call(f32[1,128,128]{2,1,0:T(8,128)S(1)} %get-tuple-element.143), custom_call_target="InvertDiagBlocksLowerTriangular" | custom-call | tf_op jit(solution)/shard_map/jit(cholesky)/cholesky | solution.py:274
  299.7 11.7 %cholesky.280 = f32[128,128]{1,0:T(8,128)S(1)} custom-call(f32[128,128]{1,0:T(8,128)S(1)} %cholesky.322), custom_call_target="Cholesky" | custom-call | tf_op jit(solution)/shard_map/jit(cholesky)/cholesky | solution.py:274
  311.4 9.8 %custom-call.33 = f32[1,128,128]{1,2,0:T(8,128)S(1)} custom-call(f32[1,128,128]{2,1,0:T(8,128)S(1)} %get-tuple-element.140), custom_call_target="InvertDiagBlocksLowerTriangular" | custom-call | tf_op jit(solution)/shard_map/jit(cholesky)/cholesky | solution.py:274
  321.8 11.7 %cholesky.299 = f32[128,128]{1,0:T(8,128)S(1)} custom-call(f32[128,128]{1,0:T(8,128)S(1)} %convolution_subtract_fusion.7), custom_call_target="Cholesky" | custom-call | tf_op jit(solution)/shard_map/jit(cholesky)/cholesky | solution.py:274
  337.5 6.0 %while.9 = (s32[]{:T(128)}, f32[384,384]{1,0:T(8,128)S(1)}, s32[3,2]{0,1:T(2,128)S(1)}, f32[3,128,128]{2,1,0:T(8,128)S(1)}, s32[]{:T(128)}) while((s32[]{:T(128)}, f32[384,384]{1,0:T(8,128)S(1)}, s32[3,2]{0,1:T(2,128)S(1)}, f32[3,128,128]{2,1,0:T(8,128)S(1)}, s32[]{:T(128)}) %tuple.92), condition=%wide.while_cond.1, body=%wide.while_body.1.sunk | while | flops 2 | bytes 131189 | solution.py:250
  338.2 1.3 bitcast_dynamic-update-slice_fusion.19
  340.2 1.3 bitcast_dynamic-update-slice_fusion.19
  342.2 1.3 bitcast_dynamic-update-slice_fusion.19
  344.2 30.5 %custom-call.35 = f32[3,128,128]{1,2,0:T(8,128)S(1)} custom-call(f32[3,128,128]{2,1,0:T(8,128)} %copy-done.13), custom_call_target="InvertDiagBlocksLowerTriangular" | custom-call | tf_op jit(solution)/shard_map/triangular_solve/custom-call.8 | solution.py:250
  374.8 1.7 fusion.3
  381.3 1.1 convolution_add_fusion.1
  382.4 1.7 convolution_add_fusion
  (183 shorter events, 46.0 us)
Async XLA Ops:
  5.1 0.9 copy-start
  155.9 1.9 copy-start.14
  160.1 0.8 copy-start.10
  220.3 2.6 copy-start.6
  231.2 39.9 %copy-start.2 = (f32[384,384]{0,1:T(8,128)}, f32[384,384]{0,1:T(8,128)S(1)}, u32[]{:S(2)}) copy-start(f32[384,384]{0,1:T(8,128)S(1)} %get-tuple-element.242) | copy-start | bytes 1769476
  262.4 0.7 copy-start.9
  271.1 4.6 %copy-start.11 = (f32[128,384]{0,1:T(8,128)S(1)}, f32[128,384]{0,1:T(8,128)}, u32[]{:S(2)}) copy-start(f32[128,384]{0,1:T(8,128)} %copy.117) | copy-start | bytes 589828
  271.1 4.6 %copy-start.12 = (f32[128,384]{0,1:T(8,128)S(1)}, f32[128,384]{0,1:T(8,128)}, u32[]{:S(2)}) copy-start(f32[128,384]{0,1:T(8,128)} %copy.116) | copy-start | bytes 589828
  274.9 0.8 copy-start.7
  289.0 85.7 %copy-start.15 = (f32[2,384]{1,0:T(2,128)S(1)}, f32[2,384]{1,0:T(2,128)}, u32[]{:S(2)}) copy-start(f32[2,384]{1,0:T(2,128)} %param.11) | copy-start | bytes 9220
  321.5 57.1 %copy-start.8 = (f32[384,384]{0,1:T(8,128)S(1)}, f32[384,384]{0,1:T(8,128)}, u32[]{:S(2)}) copy-start(f32[384,384]{0,1:T(8,128)} %copy-done.7) | copy-start | bytes 1769476
  337.4 42.0 %copy-start.3 = (f32[384,384]{0,1:T(8,128)S(1)}, f32[384,384]{0,1:T(8,128)}, u32[]{:S(2)}) copy-start(f32[384,384]{0,1:T(8,128)} %copy-done.2) | copy-start | bytes 1769476
  337.5 43.8 %copy-start.1 = (f32[32,640]{1,0:T(8,128)S(1)}, f32[32,640]{1,0:T(8,128)}, u32[]{:S(2)}) copy-start(f32[32,640]{1,0:T(8,128)} %x_ref.1) | copy-start | bytes 245764
  337.5 43.8 %copy-start.5 = (f32[384,5,128]{0,2,1:T(8,128)S(1)}, f32[384,5,128]{0,2,1:T(8,128)}, u32[]{:S(2)}) copy-start(f32[384,5,128]{0,2,1:T(8,128)} %get-tuple-element.115) | copy-start | bytes 2949124
  343.5 0.7 copy-start.13
  376.5 5.9 %copy-start.4 = (f32[384,5,128]{0,2,1:T(8,128)S(1)}, f32[384,5,128]{0,2,1:T(8,128)}, u32[]{:S(2)}) copy-start(f32[384,5,128]{0,2,1:T(8,128)} %get-tuple-element.114) | copy-start | bytes 2949124

commit v2 on v1

--- a/solution.py
+++ b/solution.py
@@ -32,8 +32,51 @@
     return out
 
 
-def gather_kernel(
-    x_ref, l_ref, oa_ref, mean_ref, gram_ref, cross_ref,
+def eliminate(ref, at):
+    spread = functools.partial(jnp.broadcast_to, shape=(8, 128))
+    lane = lax.broadcasted_iota(jnp.int32, (8, 128), 1)
+    sub = lax.broadcasted_iota(jnp.int32, (8, 128), 0)
+    a = [ref[at + 8 * i : at + 8 * i + 8, at : at + 128] for i in range(16)]
+    for p in range(16):
+        rows = a[p]
+        cols = [spread(rows[:, 8 * p + j : 8 * p + j + 1]) for j in range(8)]
+        for k in range(8):
+            col = cols[k]
+            pivot = 1.0 / spread(col[k : k + 1])
+            rows = jnp.where(lane == 8 * p + k, jnp.where(sub == k, 1.0, 0.0), rows)
+            times = jnp.where(sub == k, 1.0 - pivot, col * pivot)
+            for j in range(k + 1, 8):
+                cols[j] = cols[j] - times * spread(cols[j][k : k + 1])
+            rows = rows - times * spread(rows[k : k + 1])
+        each = [spread(rows[j : j + 1]) for j in range(8)]
+        inside = (lane >= 8 * p) & (lane < 8 * p + 8)
+        for i in [(p + 1 + i) % 16 for i in range(15)]:
+            old = a[i]
+            t = [spread(old[:, 8 * p + j : 8 * p + j + 1]) * each[j] for j in range(8)]
+            low, high = (t[0] + t[1]) + (t[2] + t[3]), (t[4] + t[5]) + (t[6] + t[7])
+            a[i] = jnp.where(inside, 0.0, old) - (low + high)
+        a[p] = rows
+    for i in range(16):
+        ref[at + 8 * i : at + 8 * i + 8, at : at + 128] = a[i]
+
+
+def sweep(ref, p):
+    part = lambda i: slice(128 * i, 128 * i + 128)
+    eliminate(ref, 128 * p)
+    inner = ref[part(p), part(p)]
+    others = [(p + 1) % 3, (p + 2) % 3]
+    for j in others:
+        ref[part(p), part(j)] = dot(inner, ref[part(p), part(j)])
+    for i in others:
+        left = ref[part(i), part(p)]
+        for j in others:
+            ref[part(i), part(j)] -= dot(left, ref[part(p), part(j)])
+        ref[part(i), part(p)] = -dot(left, inner)
+
+
+def kernel(
+    x_ref, val_ref, var_ref, rows_ref, owner_ref, out_ref,
+    oa_ref, gram_ref, cross_ref, s1, s2, ut_ref, f_ref,
     t_in, t_z, t_y, t_s, l_src, l_in, l_mine, l_all, anom,
     g_part, g_one, g_red, g_two, c_part, c_one, c_red, c_two, c_sum,
     t_send, t_recv, l_send, l_recv, g_send, g_recv, x_send, x_recv, c_send, c_recv,
@@ -77,7 +120,14 @@
         return out
 
     x = x_ref[...]
-    lrows = l_ref[...]
+    spot = lax.broadcasted_iota(jnp.int32, (ROWS, 128), 0)
+    picked = []
+    for b in range(6):
+        lanes = slice(128 * (b % 3), 128 * (b % 3) + 128)
+        held = owner_ref[b // 3 : b // 3 + 1, b % 3 : b % 3 + 1] == s
+        want = jnp.where(held, rows_ref[b // 3 : b // 3 + 1, lanes], -1)
+        picked.append(dot(x, jnp.where(spot == want, 1.0, 0.0)))
+    lrows = jnp.concatenate(picked, axis=1)
     t_in[...] = jnp.zeros_like(t_in)
     sx = jnp.sum(x, axis=0, keepdims=True)
     sl = jnp.sum(lrows, axis=0, keepdims=True)
@@ -107,7 +157,6 @@
     arrive(la)
     arrive(ts)
     omean = total(t_s, t_s[0]) / MEMBERS
-    mean_ref[...] = omean
     for b in range(6):
         oa_ref[:, 128 * b : 128 * b + 128] = l_all[4 * b : 4 * b + 4].reshape(MINE, 128) - omean[b : b + 1]
 
@@ -162,6 +211,59 @@
         where = (lax.rem(xpos + k, 4) * 2 + core, m)
         gx.append(copy(gram_ref.at[mine], gram_ref.at[mine], x_send.at[k], x_recv.at[k], where))
     started.extend(gx)
+
+    def first_step():
+        return [
+            fan(
+                first,
+                lambda k: c_part.at[pl.ds(256 * h + 32 * hop(a, k), 32)],
+                lambda k: c_one.at[h, k],
+                c_send.at[h, 0],
+                c_recv.at[h, 0],
+            )
+            for h, (first, a, second, b) in enumerate(order)
+        ]
+
+    def second_step(before):
+        out = []
+        for h, (first, a, second, b) in enumerate(order):
+            arrive(before[h])
+            c_red[h] = total(c_one.at[h], c_part[pl.ds(256 * h + 32 * a, 32)])
+            out.append(
+                fan(
+                    second,
+                    lambda k: c_red.at[h, pl.ds(4 * hop(b, k), 4)],
+                    lambda k: c_two.at[h, k],
+                    c_send.at[h, 1],
+                    c_recv.at[h, 1],
+                )
+            )
+        return out
+
+    def third_step(before):
+        out = []
+        for h, (first, a, second, b) in enumerate(order):
+            arrive(before[h])
+            c_two[h, 0] = total(c_two.at[h], c_red[h, pl.ds(4 * b, 4)])
+            spot = pl.ds(4 * b, 4)
+            c_sum[h, spot] = c_two[h, 0]
+            out.append(
+                fan(second, lambda k: c_two.at[h, 0], lambda k: c_sum.at[h, spot], c_send.at[h, 2], c_recv.at[h, 2])
+            )
+        return out
+
+    def fourth_step(before):
+        out = []
+        for h, (first, a, second, b) in enumerate(order):
+            arrive(before[h])
+            spot = pl.ds(256 * h + 32 * a, 32)
+            cross_ref[spot] = c_sum[h]
+            out.append(
+                fan(first, lambda k: c_sum.at[h], lambda k: cross_ref.at[spot], c_send.at[h, 3], c_recv.at[h, 3])
+            )
+        return out
+
+    steps = first_step()
     gc = []
     for k in range(4):
         if k > 0:
@@ -169,71 +271,74 @@
         got = pl.ds((lax.rem(xpos + 4 - k, 4) * 2 + core) * 48, 48)
         gc.append(copy(gram_ref.at[got], gram_ref.at[got], x_send.at[4 + k], x_recv.at[4 + k], (s + 1 - 2 * core, m)))
     started.extend(gc)
-
-    c1 = []
-    for h, (first, a, second, b) in enumerate(order):
-        c1.append(
-            fan(
-                first,
-                lambda k: c_part.at[pl.ds(256 * h + 32 * hop(a, k), 32)],
-                lambda k: c_one.at[h, k],
-                c_send.at[h, 0],
-                c_recv.at[h, 0],
-            )
-        )
-    c2 = []
-    for h, (first, a, second, b) in enumerate(order):
-        arrive(c1[h])
-        c_red[h] = total(c_one.at[h], c_part[pl.ds(256 * h + 32 * a, 32)])
-        c2.append(
-            fan(
-                second,
-                lambda k: c_red.at[h, pl.ds(4 * hop(b, k), 4)],
-                lambda k: c_two.at[h, k],
-                c_send.at[h, 1],
-                c_recv.at[h, 1],
-            )
-        )
-    c3 = []
-    for h, (first, a, second, b) in enumerate(order):
-        arrive(c2[h])
-        c_two[h, 0] = total(c_two.at[h], c_red[h, pl.ds(4 * b, 4)])
-        spot = pl.ds(4 * b, 4)
-        c_sum[h, spot] = c_two[h, 0]
-        c3.append(
-            fan(second, lambda k: c_two.at[h, 0], lambda k: c_sum.at[h, spot], c_send.at[h, 2], c_recv.at[h, 2])
-        )
-    c4 = []
-    for h, (first, a, second, b) in enumerate(order):
-        arrive(c3[h])
-        spot = pl.ds(256 * h + 32 * a, 32)
-        cross_ref[spot] = c_sum[h]
-        c4.append(
-            fan(first, lambda k: c_sum.at[h], lambda k: cross_ref.at[spot], c_send.at[h, 3], c_recv.at[h, 3])
-        )
     arrive(gc)
-    arrive(c4[0])
-    arrive(c4[1])
+
+    scale = 1.0 / (MEMBERS - 1.0)
+    part = lambda i: slice(128 * i, 128 * i + 128)
+    diag = lax.broadcasted_iota(jnp.int32, (128, 128), 0) == lax.broadcasted_iota(jnp.int32, (128, 128), 1)
+
+    def gram(i, j):
+        at = 16 * BLOCKS.index((i, j))
+        return gram_ref[at : at + 16].reshape(128, 128) * scale
+
+    for i in range(3):
+        s1[part(i), part(i)] = gram(i, i) + jnp.where(diag, var_ref[0:1, part(i)], 0.0)
+        for j in range(i):
+            block = gram(i, j)
+            s1[part(i), part(j)] = block
+            s1[part(j), part(i)] = block.T
+    sweep(s1, 0)
+    sweep(s1, 1)
+    sweep(s1, 2)
+    steps = second_step(steps)
+    for i in range(3):
+        for j in range(3):
+            f_ref[part(i), part(j)] = gram(3 + i, j)
+    ut_ref[...] = dot(f_ref[...], s1[...])
+    f_ref[...] = 0.75 * f_ref[...] + (0.25 * var_ref[0:1, :]) * ut_ref[...]
+    steps = third_step(steps)
+    for i in range(3):
+        taken = dot(f_ref[part(i), :], ut_ref[0 : 128 * i + 128, :], (1, 1))
+        for j in range(i + 1):
+            block = gram(3 + i, 3 + j) - taken[:, part(j)]
+            if i == j:
+                s2[part(i), part(i)] = block + jnp.where(diag, var_ref[1:2, part(i)], 0.0)
+            else:
+                s2[part(i), part(j)] = block
+                s2[part(j), part(i)] = block.T
+    sweep(s2, 0)
+    steps = fourth_step(steps)
+    sweep(s2, 1)
+    sweep(s2, 2)
+    flat = jnp.concatenate([omean[b : b + 1] for b in range(6)], axis=1)
+    gap1, gap2 = val_ref[0:1] - flat[:, :OBS], val_ref[1:2] - flat[:, OBS:]
+    o1, o2 = oa_ref[:, :OBS], oa_ref[:, OBS:]
+    b1 = gap1 - 0.5 * o1
+    b2 = gap2 - 0.5 * o2 - dot(gap1 - 0.25 * o1, ut_ref[...], (1, 1))
+    q2 = dot(b2, s2[...])
+    q1 = dot(b1 - dot(q2, f_ref[...]), s1[...])
+    q = jnp.concatenate([q1, q2], axis=1) * scale
+    arrive(steps[0])
+    arrive(steps[1])
+    for j in range(5):
+        out_ref[:, part(j)] = x_ref[:, part(j)] + dot(q, cross_ref[96 * j : 96 * j + 96].reshape(ALL, 128))
     for c in started:
         c.wait_send()
 
 
-def gather_all(x, picked):
+def shards(state, obs_values, noise_var, obs_rows, owner):
     dma = pltpu.SemaphoreType.DMA
+    plane = lambda rows, cols: pltpu.VMEM((rows, cols), F32)
     tiles = lambda *lead: pltpu.VMEM((*lead, 8, 128), F32)
     return pl.pallas_call(
-        gather_kernel,
-        out_shape=(
-            jax.ShapeDtypeStruct((MINE, ALL), F32),
-            jax.ShapeDtypeStruct((8, 128), F32),
-            jax.ShapeDtypeStruct((384, 8, 128), F32),
-            jax.ShapeDtypeStruct((512, 8, 128), F32),
-        ),
-        in_specs=[pl.BlockSpec(memory_space=pltpu.VMEM)] * 2,
-        out_specs=[pl.BlockSpec(memory_space=pltpu.VMEM)] * 4,
+        kernel,
+        out_shape=jax.ShapeDtypeStruct((MINE, ROWS), F32),
+        in_specs=[pl.BlockSpec(memory_space=pltpu.VMEM)] * 5,
+        out_specs=pl.BlockSpec(memory_space=pltpu.VMEM),
         scratch_shapes=[
+            plane(MINE, ALL), tiles(384), tiles(512), plane(OBS, OBS), plane(OBS, OBS), plane(OBS, OBS), plane(OBS, OBS),
             pltpu.VMEM((16, 128), F32), pltpu.VMEM((SIDE, 16, 128), F32), pltpu.VMEM((SIDE, 16, 128), F32), tiles(SIDE),
-            tiles(24), tiles(SIDE, 3), tiles(3), tiles(24), pltpu.VMEM((MINE, ROWS), F32),
+            tiles(24), tiles(SIDE, 3), tiles(3), tiles(24), plane(MINE, ROWS),
             tiles(384), tiles(2, SIDE, 3), tiles(2, 3), tiles(2, SIDE, 3),
             tiles(512), tiles(2, SIDE, 32), tiles(2, 32), tiles(2, SIDE, 4), tiles(2, 32),
             dma((3, SIDE)), dma((3, SIDE)), dma((2, SIDE)), dma((2, SIDE)), dma((2, 3, SIDE)), dma((2, 3, SIDE)),
@@ -242,43 +347,7 @@
         compiler_params=pltpu.CompilerParams(
             collective_id=0, has_side_effects=True, vmem_limit_bytes=40 * 2**20
         ),
-    )(x, picked)
-
-
-def solve(factor, right):
-    half = lax.linalg.triangular_solve(factor, right, left_side=True, lower=True)
-    return lax.linalg.triangular_solve(factor, half, left_side=True, lower=True, transpose_a=True)
-
-
-def shards(state, obs_values, noise_var, obs_rows, owner):
-    s = lax.axis_index("state")
-    held = jnp.repeat(owner.reshape(-1) == s, 128)
-    picked = jnp.where(held[None, :], jnp.take(state, obs_rows.reshape(-1), axis=1), 0.0)
-    oa, means, gram, cross = gather_all(state, picked)
-    scale = 1.0 / (MEMBERS - 1.0)
-    rows = []
-    parts = gram[:336].reshape(21, 128, 128)
-    for i in range(6):
-        row = []
-        for j in range(6):
-            row.append(parts[BLOCKS.index((i, j))] if j <= i else parts[BLOCKS.index((j, i))].T)
-        rows.append(jnp.concatenate(row, axis=1))
-    gram = jnp.concatenate(rows, axis=0) * scale
-    cross = cross[:480].reshape(5, ALL, 128).transpose(1, 0, 2).reshape(ALL, ROWS) * scale
-    omean = means[:6].reshape(ALL)
-    c12, c21 = gram[:OBS, OBS:], gram[OBS:, :OBS]
-    gap = obs_values.reshape(-1) - omean
-    f1 = jnp.linalg.cholesky(gram[:OBS, :OBS] + jnp.diag(noise_var[0]))
-    u = solve(f1, c12)
-    f = 0.75 * c21 + 0.25 * dot(u * noise_var[0][:, None], jnp.eye(OBS, dtype=F32), (0, 0))
-    f2 = jnp.linalg.cholesky(gram[OBS:, OBS:] - dot(f, u) + jnp.diag(noise_var[1]))
-    g1, g2 = gap[None, :OBS], gap[None, OBS:]
-    o1, o2 = oa[:, :OBS], oa[:, OBS:]
-    b1 = g1 - 0.5 * o1
-    b2 = g2 - 0.5 * o2 - dot(g1 - 0.25 * o1, u)
-    q2 = solve(f2, b2.T).T
-    q1 = solve(f1, (b1 - dot(q2, f)).T).T
-    return state + dot(q1, cross[:OBS]) + dot(q2, cross[OBS:])
+    )(state, obs_values, noise_var, obs_rows, owner)
 
 
 def solution(mesh):

time: 389 us -> 129 us (0.33)
  the two profiles are of different devices: /device:TPU:1 before, /device:TPU:4 now
where the time goes in v2:
time: 129 us; the launch traced here: 128 us
  Pallas kernels  124 us (96%)
  local copies, waits for them, and re-layouts  4.25 us (3%)
    pallas_call x1, Pallas kernels, shards(): pl.pallas_call(kernel, out_shape=jax.ShapeDtypeStruct((MINE, ROWS), F32),...  124 us
    unnamed x11, local copies, waits for them, and re-layouts  4.25 us

profile of v2, /device:TPU:4, one launch (start us, length us, event | category | flops | bytes accessed | tf_op | source)
XLA Modules:
  0.0 128.3 jit_solution(13896422729596382374)
XLA Ops:
  0.0 0.0 copy-start
  0.0 0.9 copy-done
  0.9 0.0 copy-start.1
  0.9 0.7 copy-done.1
  1.6 0.0 copy-start.2
  1.6 0.7 copy-done.2
  2.3 0.0 copy-start.3
  2.3 0.7 copy-done.3
  2.9 0.0 copy-start.4
  2.9 0.7 copy-done.4
  3.6 124.0 %shard_map.55 = f32[32,640]{1,0:T(8,128)S(1)} custom-call(f32[32,640]{1,0:T(8,128)S(1)} %copy-done, f32[2,384]{1,0:T(2,128)S(1)} %copy-done.1, f32[2,384]{1,0:T(2,128)S(1)} %copy-done.2, s32[2,384]{1,0:T(2,128)S(1)} %copy-done.3, s32[2,3]{1,0:T(2,128)S(1)} %copy-done.4), custom_call_target="tpu_custom_call" | custom-call | tf_op jit(solution)/shard_map/pallas_call | solution.py:333
  127.7 0.6 copy.7
Async XLA Ops:
  0.0 0.9 copy-start
  0.9 0.7 copy-start.1
  1.6 0.7 copy-start.2
  2.3 0.7 copy-start.3
  2.9 0.7 copy-start.4

commit v3 on v2

v3 whole, which is shorter than its diff:
```python
import functools

import jax
import jax.numpy as jnp
from jax import lax
from jax.experimental import pallas as pl
from jax.experimental.pallas import tpu as pltpu
from jax.sharding import PartitionSpec as P

MESH = pl.DeviceIdType.MESH
F32 = jnp.float32
HIGHEST = lax.Precision.HIGHEST
SIDE = 8
OBS = 384
ALL = 2 * OBS
ROWS = 640
MINE = 32
MEMBERS = 2048
GROUP = MINE * SIDE
BLOCKS = [(i, j) for i in range(6) for j in range(i + 1)]
HALVES = (0, 1)


def dot(a, b, over=(1, 0)):
    return lax.dot_general(
        a, b, (((over[0],), (over[1],)), ((), ())), precision=HIGHEST, preferred_element_type=F32
    )


def total(slots, own):
    out = own
    for k in range(1, SIDE):
        out = out + slots[k]
    return out


def eliminate(ref, at):
    spread = functools.partial(jnp.broadcast_to, shape=(8, 128))
    lane = lax.broadcasted_iota(jnp.int32, (8, 128), 1)
    sub = lax.broadcasted_iota(jnp.int32, (8, 128), 0)
    a = [ref[at + 8 * i : at + 8 * i + 8, at : at + 128] for i in range(16)]
    for p in range(16):
        rows = a[p]
        cols = [spread(rows[:, 8 * p + j : 8 * p + j + 1]) for j in range(8)]
        for k in range(8):
            col = cols[k]
            pivot = 1.0 / spread(col[k : k + 1])
            rows = jnp.where(lane == 8 * p + k, jnp.where(sub == k, 1.0, 0.0), rows)
            times = jnp.where(sub == k, 1.0 - pivot, col * pivot)
            for j in range(k + 1, 8):
                cols[j] = cols[j] - times * spread(cols[j][k : k + 1])
            rows = rows - times * spread(rows[k : k + 1])
        each = [spread(rows[j : j + 1]) for j in range(8)]
        inside = (lane >= 8 * p) & (lane < 8 * p + 8)
        for i in [(p + 1 + i) % 16 for i in range(15)]:
            old = a[i]
            t = [spread(old[:, 8 * p + j : 8 * p + j + 1]) * each[j] for j in range(8)]
            low, high = (t[0] + t[1]) + (t[2] + t[3]), (t[4] + t[5]) + (t[6] + t[7])
            a[i] = jnp.where(inside, 0.0, old) - (low + high)
        a[p] = rows
    for i in range(16):
        ref[at + 8 * i : at + 8 * i + 8, at : at + 128] = a[i]


def sweep(ref, p):
    part = lambda i: slice(128 * i, 128 * i + 128)
    eliminate(ref, 128 * p)
    inner = ref[part(p), part(p)]
    others = [(p + 1) % 3, (p + 2) % 3]
    for j in others:
        ref[part(p), part(j)] = dot(inner, ref[part(p), part(j)])
    for i in others:
        left = ref[part(i), part(p)]
        for j in others:
            ref[part(i), part(j)] -= dot(left, ref[part(p), part(j)])
        ref[part(i), part(p)] = -dot(left, inner)


def kernel(
    x_hbm, val_hbm, var_hbm, rows_hbm, owner_hbm, out_hbm,
    x_ref, val_ref, var_ref, rows_ref, owner_ref, out_ref,
    oa_ref, anom, s1, s2, ut_ref, f_ref, extra,
    t_in, t_z, t_y, t_s, t_all, l_src, l_in, l_mine, l_all,
    p_part, p_one, p_two, p_red, p_sum, r_part, r_one, r_two, r_red, r_sum,
    c_part, c_one, c_red, c_two, c_sum, cross_ref,
    in_sem, t_send, t_recv, l_send, l_recv, p_send, p_recv, r_send, r_recv, x_send, x_recv, c_send, c_recv,
):
    s = lax.axis_index("state")
    m = lax.axis_index("member")
    z, y = lax.div(m, SIDE), lax.rem(m, SIDE)
    xpos, core = lax.div(s, 2), lax.rem(s, 2)

    def hop(v, k):
        return lax.rem(v + k, SIDE)

    def peer(axis, k):
        if axis == "z":
            return (s, hop(z, k) * SIDE + y)
        if axis == "y":
            return (s, z * SIDE + hop(y, k))
        return (hop(s, k), m)

    loads = []
    pairs = ((x_hbm, x_ref), (rows_hbm, rows_ref), (owner_hbm, owner_ref), (val_hbm, val_ref), (var_hbm, var_ref))
    for i, (src, dst) in enumerate(pairs):
        c = pltpu.make_async_copy(src, dst, in_sem.at[i])
        c.start()
        loads.append(c)
    barrier = pltpu.get_barrier_semaphore()
    for axis in ("z", "y", "s"):
        for k in range(1, SIDE):
            pl.semaphore_signal(barrier, inc=1, device_id=peer(axis, k), device_id_type=MESH)

    started = []

    def copy(src, dst, send, recv, where):
        c = pltpu.make_async_remote_copy(
            src_ref=src, dst_ref=dst, send_sem=send, recv_sem=recv, device_id=where, device_id_type=MESH
        )
        c.start()
        started.append(c)
        return c

    def arrive(copies):
        for c in copies:
            c.wait_recv()

    def fan(axis, src, dst, send, recv, over=range(1, SIDE)):
        return [copy(src(k), dst(k), send.at[k], recv.at[k], peer(axis, k)) for k in over]

    for c in loads:
        c.wait()
    x = x_ref[...]
    iota = lax.broadcasted_iota(jnp.int32, (ROWS, 128), 0)
    t_in[...] = jnp.zeros_like(t_in)
    for b in range(6):
        lanes = slice(128 * (b % 3), 128 * (b % 3) + 128)
        held = owner_ref[b // 3 : b // 3 + 1, b % 3 : b % 3 + 1] == s
        want = jnp.where(held, rows_ref[b // 3 : b // 3 + 1, lanes], -1)
        rows = dot(x, jnp.where(iota == want, 1.0, 0.0))
        t_in[b : b + 1, :] = jnp.sum(rows, axis=0, keepdims=True)
        l_src[4 * b : 4 * b + 4] = rows.reshape(4, 8, 128)
    sx = jnp.sum(x, axis=0, keepdims=True)
    for b in range(5):
        t_in[8 + b : 9 + b, :] = sx[:, 128 * b : 128 * b + 128]
    pl.semaphore_wait(barrier, 3 * (SIDE - 1))

    tz = fan("z", lambda k: t_in, lambda k: t_z.at[k], t_send.at[0], t_recv.at[0])
    ls = fan("s", lambda k: l_src.at[pl.ds(3 * hop(s, k), 3)], lambda k: l_in.at[k], l_send.at[0], l_recv.at[0])
    arrive(ls)
    l_mine[...] = total(l_in, l_src[pl.ds(3 * s, 3)])
    l_all[pl.ds(3 * s, 3)] = l_mine[...]
    la = fan("s", lambda k: l_mine, lambda k: l_all.at[pl.ds(3 * s, 3)], l_send.at[1], l_recv.at[1])
    arrive(tz)
    t_y[0] = total(t_z, t_in[...])
    ts = fan("s", lambda k: t_y.at[0, 0:8], lambda k: t_s.at[k], t_send.at[1], t_recv.at[1])
    ty = fan("y", lambda k: t_y.at[0], lambda k: t_y.at[k], t_send.at[2], t_recv.at[2])
    xnear = t_y[0, 8:16] * (1.0 / GROUP)
    for b in range(5):
        anom[:, 128 * b : 128 * b + 128] = x[:, 128 * b : 128 * b + 128] - xnear[b : b + 1]
    arrive(la)
    arrive(ts)
    onear = total(t_s, t_y[0, 0:8]) * (1.0 / GROUP)
    for b in range(6):
        oa_ref[:, 128 * b : 128 * b + 128] = l_all[4 * b : 4 * b + 4].reshape(MINE, 128) - onear[b : b + 1]

    order = (("z", z, "y", y), ("y", y, "z", z))

    class Gram:
        def __init__(self, n, part, one, two, red, out, send, recv, at):
            self.n, self.part, self.one, self.two, self.red, self.out = n, part, one, two, red, out
            self.send, self.recv, self.at = send, recv, at
            self.base = s * (16 * n)

        def piece(self, h, place):
            return pl.ds(self.base + 8 * self.n * h + self.n * place, self.n)

        def scatter(self):
            self.now = [
                fan(
                    order[h][0],
                    lambda k: self.part.at[self.piece(h, hop(order[h][1], k))],
                    lambda k: self.one.at[h, k],
                    self.send.at[h, 0],
                    self.recv.at[h, 0],
                )
                for h in HALVES
            ]

        def exchange(self):
            after = []
            for h in HALVES:
                arrive(self.now[h])
                self.two[h, 0] = total(self.one.at[h], self.part[self.piece(h, order[h][1])])
                after.append(
                    fan(
                        order[h][2],
                        lambda k: self.two.at[h, 0],
                        lambda k: self.two.at[h, k],
                        self.send.at[h, 1],
                        self.recv.at[h, 1],
                    )
                )
            self.now = after

        def gather(self):
            after = []
            for h in HALVES:
                arrive(self.now[h])
                self.red[h] = total(self.two.at[h], self.two[h, 0])
                piece = self.piece(h, order[h][1])
                self.out[piece] = self.red[h]
                after.append(
                    fan(
                        order[h][0],
                        lambda k: self.red.at[h],
                        lambda k: self.out.at[piece],
                        self.send.at[h, 2],
                        self.recv.at[h, 2],
                    )
                )
            self.now = after

        def spread_chips(self):
            arrive(self.now[0] + self.now[1])
            mine = self.out.at[pl.ds(self.base, 16 * self.n)]
            self.now = [
                copy(mine, mine, x_send.at[self.at, k], x_recv.at[self.at, k], (lax.rem(xpos + k, 4) * 2 + core, m))
                for k in range(1, 4)
            ]

        def spread_cores(self):
            after = []
            for k in range(4):
                if k > 0:
                    self.now[k - 1].wait_recv()
                got = self.out.at[pl.ds((lax.rem(xpos + 4 - k, 4) * 2 + core) * (16 * self.n), 16 * self.n)]
                after.append(
                    copy(got, got, x_send.at[self.at, 4 + k], x_recv.at[self.at, 4 + k], (s + 1 - 2 * core, m))
                )
            self.now = after

        def finish(self):
            arrive(self.now)

    first = Gram(1, p_part, p_one, p_two, p_red, p_sum, p_send, p_recv, 0)
    rest = Gram(2, r_part, r_one, r_two, r_red, r_sum, r_send, r_recv, 1)

    def bands(which, into, skip):
        for i in which:
            band = dot(oa_ref[:, 128 * i : 128 * i + 128], oa_ref[:, 0 : 128 * i + 128], (0, 0))
            for j in range(i + 1):
                at = 16 * (BLOCKS.index((i, j)) - skip)
                into[at : at + 16] = band[:, 128 * j : 128 * j + 128].reshape(16, 8, 128)

    bands(range(3), p_part, 0)
    p_part[96:128] = jnp.zeros((32, 8, 128), F32)
    first.scatter()
    bands(range(3, 6), r_part, 6)
    r_part[240:256] = jnp.zeros((16, 8, 128), F32)
    for i in range(6):
        band = dot(oa_ref[:, 128 * i : 128 * i + 128], anom[...], (0, 0))
        for j in range(5):
            at = 96 * j + 16 * i
            c_part[at : at + 16] = band[:, 128 * j : 128 * j + 128].reshape(16, 8, 128)
    c_part[480:512] = jnp.zeros((32, 8, 128), F32)

    cross_steps = [[], []]

    def cross_scatter(over):
        for h in HALVES:
            cross_steps[h] += fan(
                order[h][0],
                lambda k: c_part.at[pl.ds(256 * h + 32 * hop(order[h][1], k), 32)],
                lambda k: c_one.at[h, k],
                c_send.at[h, 0],
                c_recv.at[h, 0],
                over,
            )

    def cross_second():
        for h in HALVES:
            arrive(cross_steps[h])
            c_red[h] = total(c_one.at[h], c_part[pl.ds(256 * h + 32 * order[h][1], 32)])
            cross_steps[h] = fan(
                order[h][2],
                lambda k: c_red.at[h, pl.ds(4 * hop(order[h][3], k), 4)],
                lambda k: c_two.at[h, k],
                c_send.at[h, 1],
                c_recv.at[h, 1],
            )

    def cross_third():
        for h in HALVES:
            arrive(cross_steps[h])
            spot = pl.ds(4 * order[h][3], 4)
            c_two[h, 0] = total(c_two.at[h], c_red[h, spot])
            c_sum[h, spot] = c_two[h, 0]
            cross_steps[h] = fan(
                order[h][2], lambda k: c_two.at[h, 0], lambda k: c_sum.at[h, spot], c_send.at[h, 2], c_recv.at[h, 2]
            )

    def cross_fourth():
        for h in HALVES:
            arrive(cross_steps[h])
            spot = pl.ds(256 * h + 32 * order[h][1], 32)
            cross_ref[spot] = c_sum[h]
            cross_steps[h] = fan(
                order[h][0], lambda k: c_sum.at[h], lambda k: cross_ref.at[spot], c_send.at[h, 3], c_recv.at[h, 3]
            )

    cross_scatter((1, 7))
    first.exchange()
    rest.scatter()
    arrive(ty)
    ta = fan("s", lambda k: t_y.at[:, 0:8], lambda k: t_all.at[k], t_send.at[3], t_recv.at[3])
    cross_scatter((2, 6))
    first.gather()
    rest.exchange()
    cross_scatter((3, 5))

    arrive(ta)
    obs_means = total(t_all, t_y[:, 0:8]) * (1.0 / GROUP)
    flat = jnp.concatenate([obs_means[:, b, :] for b in range(6)], axis=1)
    near = flat[0:1]
    omean = jnp.mean(flat, axis=0, keepdims=True)
    apart = flat - omean
    row_means = jnp.concatenate([t_y[:, 8 + b, :] for b in range(5)], axis=1) * (1.0 / GROUP)
    row_apart = row_means - jnp.mean(row_means, axis=0, keepdims=True)
    for i in range(6):
        band = dot(apart[:, 128 * i : 128 * i + 128] * float(GROUP), apart[:, 0 : 128 * i + 128], (0, 0))
        for j in range(i + 1):
            at = 16 * BLOCKS.index((i, j))
            extra[at : at + 16] = band[:, 128 * j : 128 * j + 128].reshape(16, 8, 128)

    first.spread_chips()
    rest.gather()
    cross_scatter((4,))
    first.spread_cores()
    first.finish()

    scale = 1.0 / (MEMBERS - 1.0)
    part = lambda i: slice(128 * i, 128 * i + 128)
    diag = lax.broadcasted_iota(jnp.int32, (128, 128), 0) == lax.broadcasted_iota(jnp.int32, (128, 128), 1)

    def gram(i, j):
        at = 16 * BLOCKS.index((i, j))
        tiles = p_sum[at : at + 16] if at < 96 else r_sum[at - 96 : at - 80]
        return ((tiles + extra[at : at + 16]) * scale).reshape(128, 128)

    for i in range(3):
        s1[part(i), part(i)] = gram(i, i) + jnp.where(diag, var_ref[0:1, part(i)], 0.0)
        for j in range(i):
            block = gram(i, j)
            s1[part(i), part(j)] = block
            s1[part(j), part(i)] = block.T
    rest.spread_chips()
    sweep(s1, 0)
    cross_second()
    rest.spread_cores()
    sweep(s1, 1)
    cross_third()
    sweep(s1, 2)
    cross_fourth()
    rest.finish()
    for i in range(3):
        for j in range(3):
            f_ref[part(i), part(j)] = gram(3 + i, j)
    ut_ref[...] = dot(f_ref[...], s1[...])
    f_ref[...] = 0.75 * f_ref[...] + (0.25 * var_ref[0:1, :]) * ut_ref[...]
    for i in range(3):
        taken = dot(f_ref[part(i), :], ut_ref[0 : 128 * i + 128, :], (1, 1))
        for j in range(i + 1):
            block = gram(3 + i, 3 + j) - taken[:, part(j)]
            if i == j:
                s2[part(i), part(i)] = block + jnp.where(diag, var_ref[1:2, part(i)], 0.0)
            else:
                s2[part(i), part(j)] = block
                s2[part(j), part(i)] = block.T
    for p in range(3):
        sweep(s2, p)
    gap = jnp.concatenate([val_ref[0:1], val_ref[1:2]], axis=1) - omean
    about = oa_ref[...] + (near - omean)
    gap1, gap2, o1, o2 = gap[:, :OBS], gap[:, OBS:], about[:, :OBS], about[:, OBS:]
    b1 = gap1 - 0.5 * o1
    b2 = gap2 - 0.5 * o2 - dot(gap1 - 0.25 * o1, ut_ref[...], (1, 1))
    q2 = dot(b2, s2[...])
    q1 = dot(b1 - dot(q2, f_ref[...]), s1[...])
    q = jnp.concatenate([q1, q2], axis=1) * scale
    low = dot(q, apart, (1, 1)) * float(GROUP)
    arrive(cross_steps[0] + cross_steps[1])
    for j in range(5):
        block = cross_ref[96 * j : 96 * j + 96].reshape(ALL, 128)
        out_ref[:, part(j)] = x_ref[:, part(j)] + (dot(q, block) + dot(low, row_apart[:, part(j)]))
    done = pltpu.make_async_copy(out_ref, out_hbm, in_sem.at[5])
    done.start()
    for c in started:
        c.wait_send()
    done.wait()


def shards(state, obs_values, noise_var, obs_rows, owner):
    dma = pltpu.SemaphoreType.DMA
    plane = lambda rows, cols: pltpu.VMEM((rows, cols), F32)
    tiles = lambda *lead: pltpu.VMEM((*lead, 8, 128), F32)
    return pl.pallas_call(
        kernel,
        out_shape=jax.ShapeDtypeStruct((MINE, ROWS), F32),
        in_specs=[pl.BlockSpec(memory_space=pl.ANY)] * 5,
        out_specs=pl.BlockSpec(memory_space=pl.ANY),
        scratch_shapes=[
            plane(MINE, ROWS), plane(2, OBS), plane(2, OBS), pltpu.VMEM((2, OBS), jnp.int32), pltpu.VMEM((2, 3), jnp.int32),
            plane(MINE, ROWS),
            plane(MINE, ALL), plane(MINE, ROWS), plane(OBS, OBS), plane(OBS, OBS), plane(OBS, OBS), plane(OBS, OBS), tiles(336),
            plane(16, 128), pltpu.VMEM((SIDE, 16, 128), F32), pltpu.VMEM((SIDE, 16, 128), F32), tiles(SIDE), tiles(SIDE, SIDE),
            tiles(24), tiles(SIDE, 3), tiles(3), tiles(24),
            tiles(128), tiles(2, SIDE, 1), tiles(2, SIDE, 1), tiles(2, 1), tiles(128),
            tiles(256), tiles(2, SIDE, 2), tiles(2, SIDE, 2), tiles(2, 2), tiles(256),
            tiles(512), tiles(2, SIDE, 32), tiles(2, 32), tiles(2, SIDE, 4), tiles(2, 32), tiles(512),
            dma((6,)), dma((4, SIDE)), dma((4, SIDE)), dma((2, SIDE)), dma((2, SIDE)),
            dma((2, 3, SIDE)), dma((2, 3, SIDE)), dma((2, 3, SIDE)), dma((2, 3, SIDE)),
            dma((2, SIDE)), dma((2, SIDE)), dma((2, 4, SIDE)), dma((2, 4, SIDE)),
        ],
        compiler_params=pltpu.CompilerParams(
            collective_id=0, has_side_effects=True, vmem_limit_bytes=60 * 2**20
        ),
    )(state, obs_values, noise_var, obs_rows, owner)


def solution(mesh):
    placed = (P("member", "state"), P(), P(), P(), P())
    return jax.shard_map(
        shards, mesh=mesh, in_specs=placed, out_specs=P("member", "state"), check_vma=False
    )
```

time: 129 us -> 113 us (0.88)
  the two profiles are of different devices: /device:TPU:4 before, /device:TPU:64 now
where the time goes in v3:
time: 113 us
  Pallas kernels  111 us (98%)
  local copies, waits for them, and re-layouts  1.53 us (1%)
    pallas_call x1, Pallas kernels, shards(): pl.pallas_call(kernel, out_shape=jax.ShapeDtypeStruct((MINE, ROWS), F32),...  111 us

profile of v3, /device:TPU:64, one launch (start us, length us, event | category | flops | bytes accessed | tf_op | source)
XLA Modules:
  0.0 112.6 jit_solution(11820731156220337625)
XLA Ops:
  0.0 111.0 %shard_map.55 = f32[32,640]{1,0:T(8,128)} custom-call(f32[32,640]{1,0:T(8,128)} %x_hbm.1, f32[2,384]{1,0:T(2,128)} %val_hbm.1, f32[2,384]{1,0:T(2,128)} %var_hbm.1, s32[2,384]{1,0:T(2,128)} %rows_hbm.1, s32[2,3]{1,0:T(2,128)} %owner_hbm.1), custom_call_target="tpu_custom_call" | custom-call | tf_op jit(solution)/shard_map/pallas_call | solution.py:406
  111.0 1.5 %copy.7 = f32[32,640]{1,0:T(8,128)} copy(f32[32,640]{1,0:T(8,128)} %shard_map.55) | data formatting | bytes 163840

commit v4 on v3

--- a/solution.py
+++ b/solution.py
@@ -17,6 +17,7 @@
 MINE = 32
 MEMBERS = 2048
 GROUP = MINE * SIDE
+SHARE = ROWS // SIDE
 BLOCKS = [(i, j) for i in range(6) for j in range(i + 1)]
 HALVES = (0, 1)
 
@@ -79,11 +80,11 @@
 def kernel(
     x_hbm, val_hbm, var_hbm, rows_hbm, owner_hbm, out_hbm,
     x_ref, val_ref, var_ref, rows_ref, owner_ref, out_ref,
-    oa_ref, anom, s1, s2, ut_ref, f_ref, extra,
+    oa_ref, s1, s2, ut_ref, f_ref, extra,
     t_in, t_z, t_y, t_s, t_all, l_src, l_in, l_mine, l_all,
     p_part, p_one, p_two, p_red, p_sum, r_part, r_one, r_two, r_red, r_sum,
-    c_part, c_one, c_red, c_two, c_sum, cross_ref,
-    in_sem, t_send, t_recv, l_send, l_recv, p_send, p_recv, r_send, r_recv, x_send, x_recv, c_send, c_recv,
+    o_big, o_mat, a_src, a_in, c_part, c_one, c_red, c_sum, d_src, d_in,
+    in_sem, t_send, t_recv, l_send, l_recv, p_send, p_recv, r_send, r_recv, x_send, x_recv, o_send, o_recv, c_send, c_recv,
 ):
     s = lax.axis_index("state")
     m = lax.axis_index("member")
@@ -151,13 +152,13 @@
     l_mine[...] = total(l_in, l_src[pl.ds(3 * s, 3)])
     l_all[pl.ds(3 * s, 3)] = l_mine[...]
     la = fan("s", lambda k: l_mine, lambda k: l_all.at[pl.ds(3 * s, 3)], l_send.at[1], l_recv.at[1])
+    mine = pl.ds(3 * s, 3)
+    o_big[0, mine] = l_mine[...]
+    ya = fan("y", lambda k: l_mine, lambda k: o_big.at[k, mine], o_send.at[0], o_recv.at[0])
     arrive(tz)
     t_y[0] = total(t_z, t_in[...])
     ts = fan("s", lambda k: t_y.at[0, 0:8], lambda k: t_s.at[k], t_send.at[1], t_recv.at[1])
     ty = fan("y", lambda k: t_y.at[0], lambda k: t_y.at[k], t_send.at[2], t_recv.at[2])
-    xnear = t_y[0, 8:16] * (1.0 / GROUP)
-    for b in range(5):
-        anom[:, 128 * b : 128 * b + 128] = x[:, 128 * b : 128 * b + 128] - xnear[b : b + 1]
     arrive(la)
     arrive(ts)
     onear = total(t_s, t_y[0, 0:8]) * (1.0 / GROUP)
@@ -258,84 +259,60 @@
     first.scatter()
     bands(range(3, 6), r_part, 6)
     r_part[240:256] = jnp.zeros((16, 8, 128), F32)
-    for i in range(6):
-        band = dot(oa_ref[:, 128 * i : 128 * i + 128], anom[...], (0, 0))
-        for j in range(5):
-            at = 96 * j + 16 * i
-            c_part[at : at + 16] = band[:, 128 * j : 128 * j + 128].reshape(16, 8, 128)
-    c_part[480:512] = jnp.zeros((32, 8, 128), F32)
-
-    cross_steps = [[], []]
-
-    def cross_scatter(over):
-        for h in HALVES:
-            cross_steps[h] += fan(
-                order[h][0],
-                lambda k: c_part.at[pl.ds(256 * h + 32 * hop(order[h][1], k), 32)],
-                lambda k: c_one.at[h, k],
-                c_send.at[h, 0],
-                c_recv.at[h, 0],
-                over,
-            )
-
-    def cross_second():
-        for h in HALVES:
-            arrive(cross_steps[h])
-            c_red[h] = total(c_one.at[h], c_part[pl.ds(256 * h + 32 * order[h][1], 32)])
-            cross_steps[h] = fan(
-                order[h][2],
-                lambda k: c_red.at[h, pl.ds(4 * hop(order[h][3], k), 4)],
-                lambda k: c_two.at[h, k],
-                c_send.at[h, 1],
-                c_recv.at[h, 1],
-            )
-
-    def cross_third():
-        for h in HALVES:
-            arrive(cross_steps[h])
-            spot = pl.ds(4 * order[h][3], 4)
-            c_two[h, 0] = total(c_two.at[h], c_red[h, spot])
-            c_sum[h, spot] = c_two[h, 0]
-            cross_steps[h] = fan(
-                order[h][2], lambda k: c_two.at[h, 0], lambda k: c_sum.at[h, spot], c_send.at[h, 2], c_recv.at[h, 2]
-            )
-
-    def cross_fourth():
-        for h in HALVES:
-            arrive(cross_steps[h])
-            spot = pl.ds(256 * h + 32 * order[h][1], 32)
-            cross_ref[spot] = c_sum[h]
-            cross_steps[h] = fan(
-                order[h][0], lambda k: c_sum.at[h], lambda k: cross_ref.at[spot], c_send.at[h, 3], c_recv.at[h, 3]
-            )
-
-    cross_scatter((1, 7))
-    first.exchange()
-    rest.scatter()
+    arrive(ya)
+    ox = [
+        copy(
+            o_big.at[:, mine],
+            o_big.at[:, mine],
+            o_send.at[1, k],
+            o_recv.at[1, k],
+            (lax.rem(xpos + k, 4) * 2 + core, m),
+        )
+        for k in range(1, 4)
+    ]
     arrive(ty)
     ta = fan("s", lambda k: t_y.at[:, 0:8], lambda k: t_all.at[k], t_send.at[3], t_recv.at[3])
-    cross_scatter((2, 6))
-    first.gather()
-    rest.exchange()
-    cross_scatter((3, 5))
+    row_means = sum(t_y[k, 8:16] for k in range(SIDE)) * (1.0 / MEMBERS)
+    about = x - jnp.concatenate([row_means[b : b + 1] for b in range(5)], axis=1)
+    a_src[...] = jnp.zeros_like(a_src)
+    for c in range(SIDE):
+        a_src[c, :, 0:SHARE] = about[:, SHARE * c : SHARE * c + SHARE]
+    a_in[0] = a_src[y]
+    first.exchange()
+    aa = fan("y", lambda k: a_src.at[hop(y, k)], lambda k: a_in.at[k], c_send.at[0], c_recv.at[0])
+    rest.scatter()
+    oc = []
+    for k in range(4):
+        if k > 0:
+            ox[k - 1].wait_recv()
+        got = o_big.at[:, pl.ds(3 * (lax.rem(xpos + 4 - k, 4) * 2 + core), 3)]
+        oc.append(copy(got, got, o_send.at[1, 4 + k], o_recv.at[1, 4 + k], (s + 1 - 2 * core, m)))
 
     arrive(ta)
     obs_means = total(t_all, t_y[:, 0:8]) * (1.0 / GROUP)
     flat = jnp.concatenate([obs_means[:, b, :] for b in range(6)], axis=1)
-    near = flat[0:1]
     omean = jnp.mean(flat, axis=0, keepdims=True)
     apart = flat - omean
-    row_means = jnp.concatenate([t_y[:, 8 + b, :] for b in range(5)], axis=1) * (1.0 / GROUP)
-    row_apart = row_means - jnp.mean(row_means, axis=0, keepdims=True)
     for i in range(6):
         band = dot(apart[:, 128 * i : 128 * i + 128] * float(GROUP), apart[:, 0 : 128 * i + 128], (0, 0))
         for j in range(i + 1):
             at = 16 * BLOCKS.index((i, j))
             extra[at : at + 16] = band[:, 128 * j : 128 * j + 128].reshape(16, 8, 128)
 
+    first.gather()
+    rest.exchange()
+    arrive(aa + oc)
+    for k in range(SIDE):
+        for b in range(6):
+            lanes = slice(128 * b, 128 * b + 128)
+            o_mat[32 * k : 32 * k + 32, lanes] = o_big[k, 4 * b : 4 * b + 4].reshape(MINE, 128) - omean[:, lanes]
+    c_part[60:64] = jnp.zeros((4, 8, 128), F32)
+    for b in range(6):
+        band = dot(a_in[...].reshape(GROUP, 128), o_mat[:, 128 * b : 128 * b + 128], (0, 0))
+        c_part[10 * b : 10 * b + 10] = band[0:SHARE].reshape(10, 8, 128)
     first.spread_chips()
+    c1 = fan("z", lambda k: c_part.at[pl.ds(8 * hop(z, k), 8)], lambda k: c_one.at[k], c_send.at[1], c_recv.at[1])
     rest.gather()
-    cross_scatter((4,))
     first.spread_cores()
     first.finish()
 
@@ -356,12 +333,14 @@
             s1[part(j), part(i)] = block.T
     rest.spread_chips()
     sweep(s1, 0)
-    cross_second()
     rest.spread_cores()
+    arrive(c1)
+    piece = pl.ds(8 * z, 8)
+    c_red[...] = total(c_one, c_part[piece])
+    c_sum[piece] = c_red[...]
+    c2 = fan("z", lambda k: c_red, lambda k: c_sum.at[piece], c_send.at[2], c_recv.at[2])
     sweep(s1, 1)
-    cross_third()
     sweep(s1, 2)
-    cross_fourth()
     rest.finish()
     for i in range(3):
         for j in range(3):
@@ -380,18 +359,23 @@
     for p in range(3):
         sweep(s2, p)
     gap = jnp.concatenate([val_ref[0:1], val_ref[1:2]], axis=1) - omean
-    about = oa_ref[...] + (near - omean)
-    gap1, gap2, o1, o2 = gap[:, :OBS], gap[:, OBS:], about[:, :OBS], about[:, OBS:]
-    b1 = gap1 - 0.5 * o1
-    b2 = gap2 - 0.5 * o2 - dot(gap1 - 0.25 * o1, ut_ref[...], (1, 1))
-    q2 = dot(b2, s2[...])
-    q1 = dot(b1 - dot(q2, f_ref[...]), s1[...])
-    q = jnp.concatenate([q1, q2], axis=1) * scale
-    low = dot(q, apart, (1, 1)) * float(GROUP)
-    arrive(cross_steps[0] + cross_steps[1])
-    for j in range(5):
-        block = cross_ref[96 * j : 96 * j + 96].reshape(ALL, 128)
-        out_ref[:, part(j)] = x_ref[:, part(j)] + (dot(q, block) + dot(low, row_apart[:, part(j)]))
+    arrive(c2)
+    cross = jnp.concatenate([c_sum[10 * b : 10 * b + 10].reshape(SHARE, 128) for b in range(6)], axis=1) * scale
+    v1 = dot(cross[:, :OBS], s1[...])
+    v2 = dot(cross[:, OBS:] - dot(v1, f_ref[...], (1, 1)), s2[...])
+    uv = dot(v2, ut_ref[...])
+    shift = dot(jnp.broadcast_to(gap, (8, ALL)), jnp.concatenate([v1 - uv, v2], axis=1), (1, 1))
+    spread = dot(o_mat[...], jnp.concatenate([0.5 * v1 - 0.25 * uv, 0.5 * v2], axis=1), (1, 1))
+    gain = shift[0:1] - spread
+    for k in range(SIDE):
+        d_src[k, :, 0:SHARE] = gain[32 * k : 32 * k + 32]
+        d_src[k, :, SHARE:128] = jnp.zeros((MINE, 128 - SHARE), F32)
+    d_in[y] = d_src[0]
+    back = fan("y", lambda k: d_src.at[SIDE - k], lambda k: d_in.at[y], c_send.at[3], c_recv.at[3])
+    arrive(back)
+    for c in range(SIDE):
+        lanes = slice(SHARE * c, SHARE * c + SHARE)
+        out_ref[:, lanes] = x_ref[:, lanes] + d_in[c, :, 0:SHARE]
     done = pltpu.make_async_copy(out_ref, out_hbm, in_sem.at[5])
     done.start()
     for c in started:
@@ -411,18 +395,20 @@
         scratch_shapes=[
             plane(MINE, ROWS), plane(2, OBS), plane(2, OBS), pltpu.VMEM((2, OBS), jnp.int32), pltpu.VMEM((2, 3), jnp.int32),
             plane(MINE, ROWS),
-            plane(MINE, ALL), plane(MINE, ROWS), plane(OBS, OBS), plane(OBS, OBS), plane(OBS, OBS), plane(OBS, OBS), tiles(336),
+            plane(MINE, ALL), plane(OBS, OBS), plane(OBS, OBS), plane(OBS, OBS), plane(OBS, OBS), tiles(336),
             plane(16, 128), pltpu.VMEM((SIDE, 16, 128), F32), pltpu.VMEM((SIDE, 16, 128), F32), tiles(SIDE), tiles(SIDE, SIDE),
             tiles(24), tiles(SIDE, 3), tiles(3), tiles(24),
             tiles(128), tiles(2, SIDE, 1), tiles(2, SIDE, 1), tiles(2, 1), tiles(128),
             tiles(256), tiles(2, SIDE, 2), tiles(2, SIDE, 2), tiles(2, 2), tiles(256),
-            tiles(512), tiles(2, SIDE, 32), tiles(2, 32), tiles(2, SIDE, 4), tiles(2, 32), tiles(512),
+            tiles(SIDE, 24), plane(GROUP, ALL), pltpu.VMEM((SIDE, MINE, 128), F32), pltpu.VMEM((SIDE, MINE, 128), F32),
+            tiles(64), tiles(SIDE, 8), tiles(8), tiles(64),
+            pltpu.VMEM((SIDE, MINE, 128), F32), pltpu.VMEM((SIDE, MINE, 128), F32),
             dma((6,)), dma((4, SIDE)), dma((4, SIDE)), dma((2, SIDE)), dma((2, SIDE)),
             dma((2, 3, SIDE)), dma((2, 3, SIDE)), dma((2, 3, SIDE)), dma((2, 3, SIDE)),
-            dma((2, SIDE)), dma((2, SIDE)), dma((2, 4, SIDE)), dma((2, 4, SIDE)),
+            dma((2, SIDE)), dma((2, SIDE)), dma((2, SIDE)), dma((2, SIDE)), dma((4, SIDE)), dma((4, SIDE)),
         ],
         compiler_params=pltpu.CompilerParams(
-            collective_id=0, has_side_effects=True, vmem_limit_bytes=60 * 2**20
+            collective_id=0, has_side_effects=True, vmem_limit_bytes=40 * 2**20
         ),
     )(state, obs_values, noise_var, obs_rows, owner)
 

time: 113 us -> 104 us (0.920)
  the two profiles are of different devices: /device:TPU:64 before, /device:TPU:1 now
where the time goes in v4:
time: 104 us; the launch traced here: 103 us
  Pallas kernels  99 us (95%)
  local copies, waits for them, and re-layouts  4.25 us (4%)
    pallas_call x1, Pallas kernels, shards(): pl.pallas_call(kernel, out_shape=jax.ShapeDtypeStruct((MINE, ROWS), F32),...  99 us
    unnamed x11, local copies, waits for them, and re-layouts  4.25 us

profile of v4, /device:TPU:1, one launch (start us, length us, event | category | flops | bytes accessed | tf_op | source)
XLA Modules:
  0.0 103.2 jit_solution(17100772767883901097)
XLA Ops:
  0.0 0.0 copy-start
  0.0 0.9 copy-done
  0.9 0.0 copy-start.1
  0.9 0.7 copy-done.1
  1.6 0.0 copy-start.2
  1.6 0.7 copy-done.2
  2.3 0.0 copy-start.3
  2.3 0.7 copy-done.3
  2.9 0.0 copy-start.4
  2.9 0.7 copy-done.4
  3.6 99.0 %shard_map.55 = f32[32,640]{1,0:T(8,128)S(1)} custom-call(f32[32,640]{1,0:T(8,128)S(1)} %copy-done, f32[2,384]{1,0:T(2,128)S(1)} %copy-done.1, f32[2,384]{1,0:T(2,128)S(1)} %copy-done.2, s32[2,384]{1,0:T(2,128)S(1)} %copy-done.3, s32[2,3]{1,0:T(2,128)S(1)} %copy-done.4), custom_call_target="tpu_custom_call" | custom-call | tf_op jit(solution)/shard_map/pallas_call | solution.py:390
  102.6 0.6 copy.7
Async XLA Ops:
  0.0 0.9 copy-start
  0.9 0.7 copy-start.1
  1.6 0.7 copy-start.2
  2.3 0.7 copy-start.3
  2.9 0.7 copy-start.4

commit v5 on v4

--- a/solution.py
+++ b/solution.py
@@ -126,7 +126,7 @@
         for c in copies:
             c.wait_recv()
 
-    def fan(axis, src, dst, send, recv, over=range(1, SIDE)):
+    def fan(axis, src, dst, send, recv, over=(4, 3, 5, 2, 6, 1, 7)):
         return [copy(src(k), dst(k), send.at[k], recv.at[k], peer(axis, k)) for k in over]
 
     for c in loads:
@@ -372,13 +372,15 @@
         d_src[k, :, SHARE:128] = jnp.zeros((MINE, 128 - SHARE), F32)
     d_in[y] = d_src[0]
     back = fan("y", lambda k: d_src.at[SIDE - k], lambda k: d_in.at[y], c_send.at[3], c_recv.at[3])
+    for c in started[: 1 - SIDE]:
+        c.wait_send()
     arrive(back)
     for c in range(SIDE):
         lanes = slice(SHARE * c, SHARE * c + SHARE)
         out_ref[:, lanes] = x_ref[:, lanes] + d_in[c, :, 0:SHARE]
     done = pltpu.make_async_copy(out_ref, out_hbm, in_sem.at[5])
     done.start()
-    for c in started:
+    for c in back:
         c.wait_send()
     done.wait()
 

time: 104 us -> 104 us (level)
  no operation moved by 1% of the time
where the time goes in v5:
time: 104 us
  Pallas kernels  99.4 us (96%)
  local copies, waits for them, and re-layouts  4.25 us (4%)
    pallas_call x1, Pallas kernels, shards(): pl.pallas_call(kernel, out_shape=jax.ShapeDtypeStruct((MINE, ROWS), F32),...  99.4 us
    unnamed x11, local copies, waits for them, and re-layouts  4.25 us

profile of v5, /device:TPU:1, one launch (start us, length us, event | category | flops | bytes accessed | tf_op | source)
XLA Modules:
  0.0 103.7 jit_solution(323127373138359221)
XLA Ops:
  0.0 0.0 copy-start
  0.0 0.9 copy-done
  0.9 0.0 copy-start.1
  0.9 0.7 copy-done.1
  1.6 0.0 copy-start.2
  1.6 0.7 copy-done.2
  2.3 0.0 copy-start.3
  2.3 0.7 copy-done.3
  2.9 0.0 copy-start.4
  2.9 0.7 copy-done.4
  3.6 99.4 %shard_map.55 = f32[32,640]{1,0:T(8,128)S(1)} custom-call(f32[32,640]{1,0:T(8,128)S(1)} %copy-done, f32[2,384]{1,0:T(2,128)S(1)} %copy-done.1, f32[2,384]{1,0:T(2,128)S(1)} %copy-done.2, s32[2,384]{1,0:T(2,128)S(1)} %copy-done.3, s32[2,3]{1,0:T(2,128)S(1)} %copy-done.4), custom_call_target="tpu_custom_call" | custom-call | tf_op jit(solution)/shard_map/pallas_call | solution.py:392
  103.1 0.6 copy.7
Async XLA Ops:
  0.0 0.9 copy-start
  0.9 0.7 copy-start.1
  1.6 0.7 copy-start.2
  2.3 0.7 copy-start.3
  2.9 0.7 copy-start.4

commit v6 on v5

--- a/solution.py
+++ b/solution.py
@@ -78,8 +78,8 @@
 
 
 def kernel(
-    x_hbm, val_hbm, var_hbm, rows_hbm, owner_hbm, out_hbm,
-    x_ref, val_ref, var_ref, rows_ref, owner_ref, out_ref,
+    x_hbm, small_hbm, out_hbm,
+    x_ref, small_ref, out_ref,
     oa_ref, s1, s2, ut_ref, f_ref, extra,
     t_in, t_z, t_y, t_s, t_all, l_src, l_in, l_mine, l_all,
     p_part, p_one, p_two, p_red, p_sum, r_part, r_one, r_two, r_red, r_sum,
@@ -102,7 +102,7 @@
         return (hop(s, k), m)
 
     loads = []
-    pairs = ((x_hbm, x_ref), (rows_hbm, rows_ref), (owner_hbm, owner_ref), (val_hbm, val_ref), (var_hbm, var_ref))
+    pairs = ((x_hbm, x_ref), (small_hbm, small_ref))
     for i, (src, dst) in enumerate(pairs):
         c = pltpu.make_async_copy(src, dst, in_sem.at[i])
         c.start()
@@ -132,12 +132,10 @@
     for c in loads:
         c.wait()
     x = x_ref[...]
-    iota = lax.broadcasted_iota(jnp.int32, (ROWS, 128), 0)
+    iota = lax.broadcasted_iota(jnp.int32, (ROWS, 128), 0).astype(F32)
     t_in[...] = jnp.zeros_like(t_in)
     for b in range(6):
-        lanes = slice(128 * (b % 3), 128 * (b % 3) + 128)
-        held = owner_ref[b // 3 : b // 3 + 1, b % 3 : b % 3 + 1] == s
-        want = jnp.where(held, rows_ref[b // 3 : b // 3 + 1, lanes], -1)
+        want = small_ref[4 + b // 3 : 5 + b // 3, 128 * (b % 3) : 128 * (b % 3) + 128]
         rows = dot(x, jnp.where(iota == want, 1.0, 0.0))
         t_in[b : b + 1, :] = jnp.sum(rows, axis=0, keepdims=True)
         l_src[4 * b : 4 * b + 4] = rows.reshape(4, 8, 128)
@@ -326,7 +324,7 @@
         return ((tiles + extra[at : at + 16]) * scale).reshape(128, 128)
 
     for i in range(3):
-        s1[part(i), part(i)] = gram(i, i) + jnp.where(diag, var_ref[0:1, part(i)], 0.0)
+        s1[part(i), part(i)] = gram(i, i) + jnp.where(diag, small_ref[2:3, part(i)], 0.0)
         for j in range(i):
             block = gram(i, j)
             s1[part(i), part(j)] = block
@@ -346,19 +344,19 @@
         for j in range(3):
             f_ref[part(i), part(j)] = gram(3 + i, j)
     ut_ref[...] = dot(f_ref[...], s1[...])
-    f_ref[...] = 0.75 * f_ref[...] + (0.25 * var_ref[0:1, :]) * ut_ref[...]
+    f_ref[...] = 0.75 * f_ref[...] + (0.25 * small_ref[2:3, :]) * ut_ref[...]
     for i in range(3):
         taken = dot(f_ref[part(i), :], ut_ref[0 : 128 * i + 128, :], (1, 1))
         for j in range(i + 1):
             block = gram(3 + i, 3 + j) - taken[:, part(j)]
             if i == j:
-                s2[part(i), part(i)] = block + jnp.where(diag, var_ref[1:2, part(i)], 0.0)
+                s2[part(i), part(i)] = block + jnp.where(diag, small_ref[3:4, part(i)], 0.0)
             else:
                 s2[part(i), part(j)] = block
                 s2[part(j), part(i)] = block.T
     for p in range(3):
         sweep(s2, p)
-    gap = jnp.concatenate([val_ref[0:1], val_ref[1:2]], axis=1) - omean
+    gap = jnp.concatenate([small_ref[0:1], small_ref[1:2]], axis=1) - omean
     arrive(c2)
     cross = jnp.concatenate([c_sum[10 * b : 10 * b + 10].reshape(SHARE, 128) for b in range(6)], axis=1) * scale
     v1 = dot(cross[:, :OBS], s1[...])
@@ -386,17 +384,19 @@
 
 
 def shards(state, obs_values, noise_var, obs_rows, owner):
+    held = jnp.repeat(owner == lax.axis_index("state"), 128, axis=1)
+    want = jnp.where(held, obs_rows, -1).astype(F32)
+    small = jnp.concatenate([obs_values, noise_var, want, jnp.zeros_like(want)], axis=0)
     dma = pltpu.SemaphoreType.DMA
     plane = lambda rows, cols: pltpu.VMEM((rows, cols), F32)
     tiles = lambda *lead: pltpu.VMEM((*lead, 8, 128), F32)
     return pl.pallas_call(
         kernel,
         out_shape=jax.ShapeDtypeStruct((MINE, ROWS), F32),
-        in_specs=[pl.BlockSpec(memory_space=pl.ANY)] * 5,
+        in_specs=[pl.BlockSpec(memory_space=pl.ANY)] * 2,
         out_specs=pl.BlockSpec(memory_space=pl.ANY),
         scratch_shapes=[
-            plane(MINE, ROWS), plane(2, OBS), plane(2, OBS), pltpu.VMEM((2, OBS), jnp.int32), pltpu.VMEM((2, 3), jnp.int32),
-            plane(MINE, ROWS),
+            plane(MINE, ROWS), plane(8, OBS), plane(MINE, ROWS),
             plane(MINE, ALL), plane(OBS, OBS), plane(OBS, OBS), plane(OBS, OBS), plane(OBS, OBS), tiles(336),
             plane(16, 128), pltpu.VMEM((SIDE, 16, 128), F32), pltpu.VMEM((SIDE, 16, 128), F32), tiles(SIDE), tiles(SIDE, SIDE),
             tiles(24), tiles(SIDE, 3), tiles(3), tiles(24),
@@ -412,7 +412,7 @@
         compiler_params=pltpu.CompilerParams(
             collective_id=0, has_side_effects=True, vmem_limit_bytes=40 * 2**20
         ),
-    )(state, obs_values, noise_var, obs_rows, owner)
+    )(state, small)
 
 
 def solution(mesh):

time: 104 us -> 104 us (level)
    unnamed x11 -> x12, local copies, waits for them, and re-layouts: 4.25 us -> 3.5 us
where the time goes in v6:
time: 104 us; the launch traced here: 103 us
  Pallas kernels  99.4 us (96%)
  local copies, waits for them, and re-layouts  3.58 us (3%)
    pallas_call x1, Pallas kernels, shards(): pl.pallas_call(kernel, out_shape=jax.ShapeDtypeStruct((MINE, ROWS), F32),...  99.4 us
    unnamed x12, local copies, waits for them, and re-layouts  3.5 us

profile of v6, /device:TPU:1, one launch (start us, length us, event | category | flops | bytes accessed | tf_op | source)
XLA Modules:
  0.0 103.1 jit_solution(12164767247205728853)
XLA Ops:
  0.0 0.0 copy-start.4
  0.0 0.7 copy-done.4
  0.7 0.0 copy-start.1
  0.7 0.1 broadcast_bitcast_fusion
  0.8 0.1 pad.3.clone
  0.8 0.5 copy-done.1
  1.4 0.0 copy-start.2
  1.4 0.0 copy-start.3
  1.4 0.7 copy-done.2
  2.1 0.0 copy-done.3
  2.1 0.1 maximum_maximum_fusion.small_hbm
  2.1 0.0 copy-start
  2.1 0.9 copy-done
  3.0 99.4 %shard_map.55 = f32[32,640]{1,0:T(8,128)S(1)} custom-call(f32[32,640]{1,0:T(8,128)S(1)} %copy-done, f32[8,384]{1,0:T(8,128)S(1)} %maximum_maximum_fusion.small_hbm), custom_call_target="tpu_custom_call" | custom-call | tf_op jit(solution)/shard_map/pallas_call | solution.py:393
  102.4 0.6 copy.11
  (3 shorter events, 0.0 us)
Async XLA Ops:
  0.0 0.7 copy-start.4
  0.7 0.7 copy-start.1
  1.4 0.7 copy-start.2
  1.4 0.7 copy-start.3
  2.1 0.9 copy-start
